TPU v7x, 128 devices: a whole 4x4x4 slice. The times are simulated.
128 devices in a mesh: ctx: 16 (over z, y_hi, core), tp: 8 (over x, y_lo).
Axes of the slice: x: 4, y: 4 (y_hi: 2, y_lo: 2; y = y_hi * 2 + y_lo), z: 4, core: 2. Of those that a mesh axis runs over, the one named last changes fastest.
Arguments:
- prompt: bfloat16 [8192, 5120], P('ctx'), may hold values from -6 to 6
- norm_gain: float32 [5120], replicated, may hold values from 0.1 to 1.9
- w_query: bfloat16 [5120, 8192], P(None, 'tp')
- w_key: bfloat16 [5120, 1024], P(None, 'tp')
- w_value: bfloat16 [5120, 1024], P(None, 'tp'), may hold values from -0.078125 to 0.078125
- query_gain: float32 [128], replicated, may hold values from 1.5 to 4
- key_gain: float32 [128], replicated, may hold values from 1.5 to 4
- table: bfloat16 [77824, 5120], P(('ctx', 'tp')), may hold values from -6 to 6
- sampled: int32 [16, 4], replicated, may hold values from 0 to 77823
Outputs:
- prompt_out: bfloat16 [8192, 8192], P('ctx', 'tp')
- decoded: bfloat16 [16, 4, 8192], P('ctx', None, 'tp')
All inputs are finite; a program needn't handle non-finite values.
Results may differ from a plain program's by a relative error of at most 0.012.
The roundings to bfloat16 on the way count: a program that leaves them out, or rounds other values in their place, can miss the bound.
Values may be sent and summed in bfloat16 or wider, within the bound.
A program may use at most 128 MiB of HBM per device.

v0:
```python
import math

import jax
import jax.numpy as jnp
from jax import lax
from jax.sharding import PartitionSpec as P

EPS = 1e-06
THETA = 1000000.0
NEGATIVE = -1e30


def rms_scale(values, gain):
    mean_square = jnp.mean(values * values, axis=-1, keepdims=True)
    return values * lax.rsqrt(mean_square + EPS) * gain


def rotate(values, positions):
    half = values.shape[-1] // 2
    freqs = THETA ** (-jnp.arange(half, dtype=jnp.float32) / half)
    angles = positions.astype(jnp.float32)[:, None] * freqs[None, :]
    cosine = jnp.cos(angles)[:, None, :]
    sine = jnp.sin(angles)[:, None, :]
    first = values[..., :half]
    second = values[..., half:]
    return jnp.concatenate(
        [first * cosine - second * sine, second * cosine + first * sine], axis=-1
    )


def project(hidden, positions, norm_gain, w_query, w_key, w_value, query_gain, key_gain):
    head = query_gain.shape[0]
    count = hidden.shape[0]
    normed = rms_scale(hidden, norm_gain).astype(jnp.bfloat16)
    query_raw = jnp.dot(normed, w_query, preferred_element_type=jnp.float32).reshape(
        count, -1, head
    )
    key_raw = jnp.dot(normed, w_key, preferred_element_type=jnp.float32).reshape(count, -1, head)
    values = (
        jnp.dot(normed, w_value, preferred_element_type=jnp.float32)
        .astype(jnp.bfloat16)
        .reshape(count, -1, head)
    )
    queries = rotate(rms_scale(query_raw, query_gain), positions).astype(jnp.bfloat16)
    keys = rotate(rms_scale(key_raw, key_gain), positions).astype(jnp.bfloat16)
    return (queries, keys, values)


def empty_state(kv_heads, group, count, head):
    top = jnp.full((kv_heads, group, count), NEGATIVE, jnp.float32)
    total = jnp.zeros((kv_heads, group, count), jnp.float32)
    mixed = jnp.zeros((kv_heads, group, count, head), jnp.float32)
    return (top, total, mixed)


def absorb(state, queries, keys, values, mask):
    top, total, mixed = state
    head = queries.shape[-1]
    scores = jnp.einsum(
        "qhgd,khd->hgqk", queries, keys, preferred_element_type=jnp.float32
    ) * head ** (-0.5)
    live = mask[None, None]
    new_top = jnp.maximum(top, jnp.max(jnp.where(live, scores, NEGATIVE), axis=-1))
    raw_weights = jnp.where(live, jnp.exp(scores - new_top[..., None]), 0.0)
    factor = jnp.exp(top - new_top)
    total = total * factor + jnp.sum(raw_weights, axis=-1)
    weights = raw_weights.astype(jnp.bfloat16)
    mixed = mixed * factor[..., None] + jnp.einsum(
        "hgqk,khd->hgqd", weights, values, preferred_element_type=jnp.float32
    )
    return (new_top, total, mixed)


def finish(total, mixed):
    result = jnp.transpose(mixed / total[..., None], (2, 0, 1, 3))
    return result.reshape(result.shape[0], -1).astype(jnp.bfloat16)


def body(prompt, norm_gain, w_query, w_key, w_value, query_gain, key_gain, table, sampled):
    rows = prompt.shape[0]
    head = query_gain.shape[0]
    kv_local = w_key.shape[1] // head
    q_local = w_query.shape[1] // head
    group = q_local // kv_local
    samples = lax.axis_size("ctx")
    prompt_len = rows * samples
    steps = sampled.shape[1]
    shard = lax.axis_index("ctx")
    positions = shard * rows + jnp.arange(rows, dtype=jnp.int32)
    last_own = shard * rows + rows - 1
    queries, keys, values = project(
        prompt.astype(jnp.float32),
        positions,
        norm_gain,
        w_query,
        w_key,
        w_value,
        query_gain,
        key_gain,
    )
    grouped = queries.reshape(rows, kv_local, group, head)
    flat_keys = keys.reshape(rows, kv_local * head)
    flat_values = values.reshape(rows, kv_local * head)
    vocab_rows = table.shape[0]
    first_row = lax.axis_index(("ctx", "tp")) * vocab_rows
    picks = (sampled[:, :, None] == first_row + jnp.arange(vocab_rows, dtype=jnp.int32)).astype(
        jnp.bfloat16
    )
    partial_value = jnp.einsum("stv,vd->std", picks, table, preferred_element_type=jnp.float32)
    summed = lax.psum(partial_value, ("ctx", "tp"))
    embedded = lax.dynamic_slice_in_dim(summed, shard, 1, 0)[0]
    step_pos = prompt_len + jnp.arange(steps, dtype=jnp.int32)
    step_q, step_k, step_v = project(
        embedded, step_pos, norm_gain, w_query, w_key, w_value, query_gain, key_gain
    )
    step_grouped = step_q.reshape(steps, kv_local, group, head)
    causal = (
        jnp.arange(steps, dtype=jnp.int32)[None, :] <= jnp.arange(steps, dtype=jnp.int32)[:, None]
    )
    prompt_init = empty_state(kv_local, group, rows, head)
    fold_init = (prompt_init,)
    state = fold_init
    piece_keys = lax.all_gather(flat_keys, "ctx", axis=0, tiled=True)
    piece_values = lax.all_gather(flat_values, "ctx", axis=0, tiled=True)
    count = piece_keys.shape[0]
    block = math.gcd(count, 512)
    stacked_keys = piece_keys.reshape(count // block, block, kv_local, head)
    stacked_values = piece_values.reshape(count // block, block, kv_local, head)

    def advance(carry, item):
        block_keys, block_values, number = item
        first_key = number * block
        key_pos = first_key + jnp.arange(block, dtype=jnp.int32)
        mask = key_pos[None, :] <= positions[:, None]
        prompt_state = lax.cond(
            first_key <= last_own,
            lambda c: absorb(c, grouped, block_keys, block_values, mask),
            lambda c: c,
            carry[0],
        )
        return ((prompt_state,), None)

    numbers = jnp.arange(count // block, dtype=jnp.int32)
    state, _ = lax.scan(advance, state, (stacked_keys, stacked_values, numbers))
    _, prompt_total, prompt_mixed = state[0]
    prompt_out = finish(prompt_total, prompt_mixed)
    cache_keys, cache_values = (
        lax.all_gather(flat_keys, "ctx", axis=0, tiled=True),
        lax.all_gather(flat_values, "ctx", axis=0, tiled=True),
    )
    all_keys = jnp.concatenate([cache_keys.reshape(prompt_len, kv_local, head), step_k], axis=0)
    all_values = jnp.concatenate([cache_values.reshape(prompt_len, kv_local, head), step_v], axis=0)
    mask = jnp.concatenate([jnp.ones((steps, prompt_len), dtype=bool), causal], axis=1)
    _, step_total, step_mixed = absorb(
        empty_state(kv_local, group, steps, head), step_grouped, all_keys, all_values, mask
    )
    decoded = finish(step_total, step_mixed)[None]
    return (prompt_out, decoded)


def solution(mesh):
    in_specs = (
        P("ctx", None),
        P(),
        P(None, "tp"),
        P(None, "tp"),
        P(None, "tp"),
        P(),
        P(),
        P(("ctx", "tp"), None),
        P(),
    )
    out_specs = (P("ctx", "tp"), P("ctx", None, "tp"))
    return jax.shard_map(body, mesh=mesh, in_specs=in_specs, out_specs=out_specs, check_vma=False)
```

profile of v0, /device:TPU:121, one launch (start us, length us, event | category | flops | bytes accessed | tf_op | source)
XLA Modules:
  0.0 376.3 jit_solution(9848828550398472890)
XLA Ops:
  8.1 5.2 %fusion.28 = f32[16,4,5120]{2,0,1:T(8,128)} fusion(bf16[608,5120]{1,0:T(8,128)(2,1)} %param.20, s32[608]{0:T(1024)S(1)} %iota_add_fusion, s32[16,4]{0,1:T(4,128)} %param.21), kind=kOutput, calls=%fused_computation.36 | convolution fusion | flops 398497792 | bytes 7539328 | tf_op jit(solution)/shard_map/stv,vd->std/dot_general | solution.py:109
  13.4 3.7 fusion.24
  21.1 4.8 %convolution_convert_fusion = bf16[512,128]{1,0:T(8,128)(2,1)} fusion(bf16[5120,128]{1,0:T(8,128)(2,1)S(1)} %copy-done.5, bf16[512,5120]{1,0:T(8,128)(2,1)} %param.13, f32[5120]{0:T(1024)S(1)} %copy-done.9, f32[512]{0:T(512)S(1)} %add_rsqrt_fusion.3), kind=kOutput, calls=%fused_computation.51 | convolution fusion | flops 681639936 | bytes 6707200 | tf_op jit(solution)/shard_map/dot_general | solution.py:40
  27.7 10.0 %fusion.87 = f32[512,1024]{1,0:T(8,128)S(1)} fusion(bf16[5120,1024]{1,0:T(8,128)(2,1)} %param.15, bf16[512,5120]{1,0:T(8,128)(2,1)} %param.13, f32[5120]{0:T(1024)S(1)} %copy-done.9, f32[512]{0:T(512)S(1)} %add_rsqrt_fusion.3), kind=kOutput, calls=%fused_computation.140 | convolution fusion | flops 5379194880 | bytes 17848320 | tf_op jit(solution)/shard_map/dot_general | solution.py:35
  37.7 13.8 %copy.53 = bf16[1024,5120]{1,0:T(8,128)(2,1)} copy(bf16[1024,5120]{0,1:T(8,128)(2,1)} %bitcast.158) | data formatting | bytes 20971520 | tf_op jit(solution)/shard_map/dot_general | solution.py:35
  57.0 113.1 %all-reduce.3.cloned.1.call-done = f32[16,4,5120]{2,0,1:T(8,128)} async-done(((f32[16,4,5120]{2,0,1:T(8,128)}), f32[16,4,5120]{2,0,1:T(8,128)}) %all-reduce.3.cloned.1.call-update) | async-done | bytes 1310736 | tf_op jit(solution)/shard_map/psum | solution.py:110
  173.6 5.7 %multiply_reduce_fusion.2 = (f32[4,8]{0,1:T(8,128)S(1)}, f32[4,8,128]{2,0,1:T(4,128)S(1)}) fusion(bf16[8,128,5120]{2,1,0:T(8,128)(2,1)} %bitcast.157, bf16[1,4,5120]{2,0,1:T(2,128)(2,1)S(1)} %multiply_convert_fusion), kind=kOutput, calls=%fused_computation.103 | convolution fusion | flops 41951200 | bytes 10543232 | tf_op jit(solution)/shard_map/dot_general | solution.py:35
  185.2 4.1 %copy.51 = bf16[8192,128]{1,0:T(8,128)(2,1)} copy(bf16[8192,128]{0,1:T(8,128)(2,1)} %all-gather.3.cloned.1.call-done) | data formatting | bytes 4194304
  190.7 174.1 %while.15 = (s32[]{:T(128)}, f32[1,8,512]{2,1,0:T(8,128)S(1)}, f32[1,8,512]{2,1,0:T(8,128)S(1)}, f32[1,8,512,128]{3,2,1,0:T(8,128)}, s32[16]{0:T(128)S(1)}, /*in...) while((s32[]{:T(128)}, f32[1,8,512]{2,1,0:T(8,128)S(1)}, ...), condition=%wide.region_8.9_spmd.clone, body=%wide.region_3.8_spmd.clone.sunk | while | flops 1098134528 | bytes 48776552 | solution.py:144
  192.1 9.5 %conditional.3 = ((f32[1,8,512]{2,1,0:T(8,128)S(1)}, f32[1,8,512]{2,1,0:T(8,128)S(1)}, f32[1,8,512,128]{3,2,1,0:T(8,128)})) conditional(s32[]{:T(128)} %convert_element_type.180, (f32[1,8,512]{2,1,0:T(8,128)S(1)}, f32[1,8,512]{2,1,0:T(8,128)S(1)}, f32[1,8,512,128]{3,2,1,0:T(8,128)}) %tuple.57, (s32[]{:T(128)}, s32[1,512]{1,0:T(1,128)S(1)}, s32[]{:T(128)}, ...), branch_computations={%region_4.4_spmd, %region_5.7_spmd} | conditional | flops 1098134528 | bytes 48772192 | solution.py:135
  203.0 9.5 %conditional.3 = ((f32[1,8,512]{2,1,0:T(8,128)S(1)}, f32[1,8,512]{2,1,0:T(8,128)S(1)}, f32[1,8,512,128]{3,2,1,0:T(8,128)})) conditional(s32[]{:T(128)} %convert_element_type.180, (f32[1,8,512]{2,1,0:T(8,128)S(1)}, f32[1,8,512]{2,1,0:T(8,128)S(1)}, f32[1,8,512,128]{3,2,1,0:T(8,128)}) %tuple.57, (s32[]{:T(128)}, s32[1,512]{1,0:T(1,128)S(1)}, s32[]{:T(128)}, ...), branch_computations={%region_4.4_spmd, %region_5.7_spmd} | conditional | flops 1098134528 | bytes 48772192 | solution.py:135
  207.5 3.7 bitcast_add_fusion
  213.9 9.5 %conditional.3 = ((f32[1,8,512]{2,1,0:T(8,128)S(1)}, f32[1,8,512]{2,1,0:T(8,128)S(1)}, f32[1,8,512,128]{3,2,1,0:T(8,128)})) conditional(s32[]{:T(128)} %convert_element_type.180, (f32[1,8,512]{2,1,0:T(8,128)S(1)}, f32[1,8,512]{2,1,0:T(8,128)S(1)}, f32[1,8,512,128]{3,2,1,0:T(8,128)}) %tuple.57, (s32[]{:T(128)}, s32[1,512]{1,0:T(1,128)S(1)}, s32[]{:T(128)}, ...), branch_computations={%region_4.4_spmd, %region_5.7_spmd} | conditional | flops 1098134528 | bytes 48772192 | solution.py:135
  218.3 3.7 bitcast_add_fusion
  224.7 9.5 %conditional.3 = ((f32[1,8,512]{2,1,0:T(8,128)S(1)}, f32[1,8,512]{2,1,0:T(8,128)S(1)}, f32[1,8,512,128]{3,2,1,0:T(8,128)})) conditional(s32[]{:T(128)} %convert_element_type.180, (f32[1,8,512]{2,1,0:T(8,128)S(1)}, f32[1,8,512]{2,1,0:T(8,128)S(1)}, f32[1,8,512,128]{3,2,1,0:T(8,128)}) %tuple.57, (s32[]{:T(128)}, s32[1,512]{1,0:T(1,128)S(1)}, s32[]{:T(128)}, ...), branch_computations={%region_4.4_spmd, %region_5.7_spmd} | conditional | flops 1098134528 | bytes 48772192 | solution.py:135
  229.2 3.7 bitcast_add_fusion
  235.6 9.5 %conditional.3 = ((f32[1,8,512]{2,1,0:T(8,128)S(1)}, f32[1,8,512]{2,1,0:T(8,128)S(1)}, f32[1,8,512,128]{3,2,1,0:T(8,128)})) conditional(s32[]{:T(128)} %convert_element_type.180, (f32[1,8,512]{2,1,0:T(8,128)S(1)}, f32[1,8,512]{2,1,0:T(8,128)S(1)}, f32[1,8,512,128]{3,2,1,0:T(8,128)}) %tuple.57, (s32[]{:T(128)}, s32[1,512]{1,0:T(1,128)S(1)}, s32[]{:T(128)}, ...), branch_computations={%region_4.4_spmd, %region_5.7_spmd} | conditional | flops 1098134528 | bytes 48772192 | solution.py:135
  240.1 3.7 bitcast_add_fusion
  246.5 9.5 %conditional.3 = ((f32[1,8,512]{2,1,0:T(8,128)S(1)}, f32[1,8,512]{2,1,0:T(8,128)S(1)}, f32[1,8,512,128]{3,2,1,0:T(8,128)})) conditional(s32[]{:T(128)} %convert_element_type.180, (f32[1,8,512]{2,1,0:T(8,128)S(1)}, f32[1,8,512]{2,1,0:T(8,128)S(1)}, f32[1,8,512,128]{3,2,1,0:T(8,128)}) %tuple.57, (s32[]{:T(128)}, s32[1,512]{1,0:T(1,128)S(1)}, s32[]{:T(128)}, ...), branch_computations={%region_4.4_spmd, %region_5.7_spmd} | conditional | flops 1098134528 | bytes 48772192 | solution.py:135
  251.0 3.7 bitcast_add_fusion
  257.4 9.5 %conditional.3 = ((f32[1,8,512]{2,1,0:T(8,128)S(1)}, f32[1,8,512]{2,1,0:T(8,128)S(1)}, f32[1,8,512,128]{3,2,1,0:T(8,128)})) conditional(s32[]{:T(128)} %convert_element_type.180, (f32[1,8,512]{2,1,0:T(8,128)S(1)}, f32[1,8,512]{2,1,0:T(8,128)S(1)}, f32[1,8,512,128]{3,2,1,0:T(8,128)}) %tuple.57, (s32[]{:T(128)}, s32[1,512]{1,0:T(1,128)S(1)}, s32[]{:T(128)}, ...), branch_computations={%region_4.4_spmd, %region_5.7_spmd} | conditional | flops 1098134528 | bytes 48772192 | solution.py:135
  261.9 3.7 bitcast_add_fusion
  268.3 9.5 %conditional.3 = ((f32[1,8,512]{2,1,0:T(8,128)S(1)}, f32[1,8,512]{2,1,0:T(8,128)S(1)}, f32[1,8,512,128]{3,2,1,0:T(8,128)})) conditional(s32[]{:T(128)} %convert_element_type.180, (f32[1,8,512]{2,1,0:T(8,128)S(1)}, f32[1,8,512]{2,1,0:T(8,128)S(1)}, f32[1,8,512,128]{3,2,1,0:T(8,128)}) %tuple.57, (s32[]{:T(128)}, s32[1,512]{1,0:T(1,128)S(1)}, s32[]{:T(128)}, ...), branch_computations={%region_4.4_spmd, %region_5.7_spmd} | conditional | flops 1098134528 | bytes 48772192 | solution.py:135
  272.7 3.7 bitcast_add_fusion
  279.1 9.5 %conditional.3 = ((f32[1,8,512]{2,1,0:T(8,128)S(1)}, f32[1,8,512]{2,1,0:T(8,128)S(1)}, f32[1,8,512,128]{3,2,1,0:T(8,128)})) conditional(s32[]{:T(128)} %convert_element_type.180, (f32[1,8,512]{2,1,0:T(8,128)S(1)}, f32[1,8,512]{2,1,0:T(8,128)S(1)}, f32[1,8,512,128]{3,2,1,0:T(8,128)}) %tuple.57, (s32[]{:T(128)}, s32[1,512]{1,0:T(1,128)S(1)}, s32[]{:T(128)}, ...), branch_computations={%region_4.4_spmd, %region_5.7_spmd} | conditional | flops 1098134528 | bytes 48772192 | solution.py:135
  290.0 9.5 %conditional.3 = ((f32[1,8,512]{2,1,0:T(8,128)S(1)}, f32[1,8,512]{2,1,0:T(8,128)S(1)}, f32[1,8,512,128]{3,2,1,0:T(8,128)})) conditional(s32[]{:T(128)} %convert_element_type.180, (f32[1,8,512]{2,1,0:T(8,128)S(1)}, f32[1,8,512]{2,1,0:T(8,128)S(1)}, f32[1,8,512,128]{3,2,1,0:T(8,128)}) %tuple.57, (s32[]{:T(128)}, s32[1,512]{1,0:T(1,128)S(1)}, s32[]{:T(128)}, ...), branch_computations={%region_4.4_spmd, %region_5.7_spmd} | conditional | flops 1098134528 | bytes 48772192 | solution.py:135
  300.9 9.5 %conditional.3 = ((f32[1,8,512]{2,1,0:T(8,128)S(1)}, f32[1,8,512]{2,1,0:T(8,128)S(1)}, f32[1,8,512,128]{3,2,1,0:T(8,128)})) conditional(s32[]{:T(128)} %convert_element_type.180, (f32[1,8,512]{2,1,0:T(8,128)S(1)}, f32[1,8,512]{2,1,0:T(8,128)S(1)}, f32[1,8,512,128]{3,2,1,0:T(8,128)}) %tuple.57, (s32[]{:T(128)}, s32[1,512]{1,0:T(1,128)S(1)}, s32[]{:T(128)}, ...), branch_computations={%region_4.4_spmd, %region_5.7_spmd} | conditional | flops 1098134528 | bytes 48772192 | solution.py:135
  311.8 9.5 %conditional.3 = ((f32[1,8,512]{2,1,0:T(8,128)S(1)}, f32[1,8,512]{2,1,0:T(8,128)S(1)}, f32[1,8,512,128]{3,2,1,0:T(8,128)})) conditional(s32[]{:T(128)} %convert_element_type.180, (f32[1,8,512]{2,1,0:T(8,128)S(1)}, f32[1,8,512]{2,1,0:T(8,128)S(1)}, f32[1,8,512,128]{3,2,1,0:T(8,128)}) %tuple.57, (s32[]{:T(128)}, s32[1,512]{1,0:T(1,128)S(1)}, s32[]{:T(128)}, ...), branch_computations={%region_4.4_spmd, %region_5.7_spmd} | conditional | flops 1098134528 | bytes 48772192 | solution.py:135
  322.7 9.5 %conditional.3 = ((f32[1,8,512]{2,1,0:T(8,128)S(1)}, f32[1,8,512]{2,1,0:T(8,128)S(1)}, f32[1,8,512,128]{3,2,1,0:T(8,128)})) conditional(s32[]{:T(128)} %convert_element_type.180, (f32[1,8,512]{2,1,0:T(8,128)S(1)}, f32[1,8,512]{2,1,0:T(8,128)S(1)}, f32[1,8,512,128]{3,2,1,0:T(8,128)}) %tuple.57, (s32[]{:T(128)}, s32[1,512]{1,0:T(1,128)S(1)}, s32[]{:T(128)}, ...), branch_computations={%region_4.4_spmd, %region_5.7_spmd} | conditional | flops 1098134528 | bytes 48772192 | solution.py:135
  333.5 9.5 %conditional.3 = ((f32[1,8,512]{2,1,0:T(8,128)S(1)}, f32[1,8,512]{2,1,0:T(8,128)S(1)}, f32[1,8,512,128]{3,2,1,0:T(8,128)})) conditional(s32[]{:T(128)} %convert_element_type.180, (f32[1,8,512]{2,1,0:T(8,128)S(1)}, f32[1,8,512]{2,1,0:T(8,128)S(1)}, f32[1,8,512,128]{3,2,1,0:T(8,128)}) %tuple.57, (s32[]{:T(128)}, s32[1,512]{1,0:T(1,128)S(1)}, s32[]{:T(128)}, ...), branch_computations={%region_4.4_spmd, %region_5.7_spmd} | conditional | flops 1098134528 | bytes 48772192 | solution.py:135
  344.4 9.5 %conditional.3 = ((f32[1,8,512]{2,1,0:T(8,128)S(1)}, f32[1,8,512]{2,1,0:T(8,128)S(1)}, f32[1,8,512,128]{3,2,1,0:T(8,128)})) conditional(s32[]{:T(128)} %convert_element_type.180, (f32[1,8,512]{2,1,0:T(8,128)S(1)}, f32[1,8,512]{2,1,0:T(8,128)S(1)}, f32[1,8,512,128]{3,2,1,0:T(8,128)}) %tuple.57, (s32[]{:T(128)}, s32[1,512]{1,0:T(1,128)S(1)}, s32[]{:T(128)}, ...), branch_computations={%region_4.4_spmd, %region_5.7_spmd} | conditional | flops 1098134528 | bytes 48772192 | solution.py:135
  355.3 9.5 %conditional.3 = ((f32[1,8,512]{2,1,0:T(8,128)S(1)}, f32[1,8,512]{2,1,0:T(8,128)S(1)}, f32[1,8,512,128]{3,2,1,0:T(8,128)})) conditional(s32[]{:T(128)} %convert_element_type.180, (f32[1,8,512]{2,1,0:T(8,128)S(1)}, f32[1,8,512]{2,1,0:T(8,128)S(1)}, f32[1,8,512,128]{3,2,1,0:T(8,128)}) %tuple.57, (s32[]{:T(128)}, s32[1,512]{1,0:T(1,128)S(1)}, s32[]{:T(128)}, ...), branch_computations={%region_4.4_spmd, %region_5.7_spmd} | conditional | flops 1098134528 | bytes 48772192 | solution.py:135
  (326 shorter events, 161.1 us)
Async XLA Ops:
  8.0 9.2 %copy-start = (bf16[5120,128]{1,0:T(8,128)(2,1)S(1)}, bf16[5120,128]{1,0:T(8,128)(2,1)}, u32[]{:S(2)}) copy-start(bf16[5120,128]{1,0:T(8,128)(2,1)} %param.16) | copy-start | bytes 3932164
  8.0 162.1 %all-reduce.3.cloned.1.call-start = ((), (), s32[]{:S(2)}) async-start(), calls=%async_computation.2 | async-start | bytes 2621440 | tf_op jit(solution)/shard_map/psum | solution.py:110
  13.3 3.9 %copy-start.9 = (f32[5120]{0:T(1024)S(1)}, f32[5120]{0:T(1024)}, u32[]{:S(2)}) copy-start(f32[5120]{0:T(1024)} %param.14) | copy-start | bytes 61444
  13.3 166.5 %all-gather.3.cloned.1.call-start = ((), (), s32[]{:S(2)}) async-start(), calls=%async_computation | async-start | bytes 2228224 | tf_op jit(solution)/shard_map/all_gather | solution.py:123
  13.4 4.0 %copy-start.4 = (bf16[512,5120]{1,0:T(8,128)(2,1)S(1)}, bf16[512,5120]{1,0:T(8,128)(2,1)}, u32[]{:S(2)}) copy-start(bf16[512,5120]{1,0:T(8,128)(2,1)} %param.13) | copy-start | bytes 15728644
  17.4 2.1 copy-start.11
  17.4 3.6 copy-start.5
  20.8 161.6 %all-gather.5.cloned.1.call-start = ((), (), s32[]{:S(2)}) async-start(), calls=%async_computation.1 | async-start | bytes 2228224 | tf_op jit(solution)/shard_map/all_gather | solution.py:124
  52.1 2.4 copy-start.10
  173.5 6.0 %copy-start.6 = (bf16[5120,128]{1,0:T(8,128)(2,1)S(1)}, bf16[5120,128]{1,0:T(8,128)(2,1)}, u32[]{:S(2)}) copy-start(bf16[5120,128]{1,0:T(8,128)(2,1)} %param.17) | copy-start | bytes 3932164
  194.8 1.8 copy-start.2
  200.3 1.3 copy-start.3
  205.7 1.8 copy-start.2
  211.2 1.3 copy-start.3
  216.6 1.8 copy-start.2
  222.1 1.3 copy-start.3
  227.4 1.8 copy-start.2
  233.0 1.3 copy-start.3
  238.3 1.8 copy-start.2
  243.8 1.3 copy-start.3
  249.2 1.8 copy-start.2
  260.1 1.8 copy-start.2
  271.0 1.8 copy-start.2
  281.8 1.8 copy-start.2
  292.7 1.8 copy-start.2
  303.6 1.8 copy-start.2
  314.5 1.8 copy-start.2
  325.4 1.8 copy-start.2
  336.2 1.8 copy-start.2
  347.1 1.8 copy-start.2
  358.0 1.8 copy-start.2
  364.8 4.0 %copy-start.1 = (bf16[5120,128]{1,0:T(8,128)(2,1)S(1)}, bf16[5120,128]{1,0:T(8,128)(2,1)}, u32[]{:S(2)}) copy-start(bf16[5120,128]{1,0:T(8,128)(2,1)} %param.16) | copy-start | bytes 3932164
  (13 other events, 16.3 us)
Sparse Core Ops, SparseCore 0:
  13.6 156.4 all-reduce.2
Sparse Core Ops, SparseCore 1:
  20.9 45.2 all-gather.2
  68.5 47.5 all-gather.4
where the time goes:
time: 378 us; the launch traced here: 376 us
  matrix products  131 us (35%)
  waiting for transfers between devices  113 us (30%)
  local copies, waits for them, and re-layouts  56.7 us (15%)
  other arithmetic  46.6 us (12%)
  between operations  15.8 us (4%)
  loops' own time  12.9 us (3%)
    psum x1, waiting for transfers between devices, body(): summed = lax.psum(partial_value, ('ctx', 'tp'))  113 us
    dot_general x17, matrix products, absorb(): jnp.einsum('hgqk,khd->hgqd', weights, values, preferred_element_type=jnp....  61.8 us
    dot_general x17, matrix products, absorb(): jnp.einsum('qhgd,khd->hgqk', queries, keys, preferred_element_type=jnp.fl...  40.6 us
    reduce_sum x17, other arithmetic, absorb(): total = total * factor + jnp.sum(raw_weights, axis=-1)  28.2 us
    cond x80, local copies, waits for them, and re-layouts  20.8 us
    dot_general x2, matrix products, project(): jnp.dot(normed, w_query, preferred_element_type=jnp.float32)  15.7 us
    dot_general x1, local copies, waits for them, and re-layouts, project(): jnp.dot(normed, w_query, preferred_element_type=jnp.float32)  13.8 us
    another operation x1, loops' own time, body(): state, _ = lax.scan(advance, state, (stacked_keys, stacked_values, numbers))  11.3 us
  transfers between devices with their start and end apart: 3, of which 1 were waited for; matrix products, arithmetic and copies ran while one was open for 15% of the time, Pallas kernels for 0%

commit v1 on v0

v1 whole, which is shorter than its diff:
```python
import functools

import jax
import jax.numpy as jnp
import numpy as np
from jax import lax
from jax.experimental import pallas as pl
from jax.experimental.pallas import tpu as pltpu
from jax.sharding import PartitionSpec as P

MESH = pl.DeviceIdType.MESH
EPS = 1e-06
THETA = 1000000.0
HD = 128
ROWS = 512
D = 5120
PAIR = 2 * ROWS
HEADS = 8
NCTX = 16
NTP = 8
VROWS = 608
PIECE = D // NTP
SCALE = HD ** (-0.5) * 1.4426950408889634
LOW = -1e30
GROUP = 10
SPARE = 12
ACC = HD + 16


def rope_tables(prompt_len):
    half = HD // 2
    freqs = THETA ** (-np.arange(half, dtype=np.float64) / half)
    freqs = np.concatenate([freqs, freqs])[None, :]
    sign = np.concatenate([-np.ones(half), np.ones(half)])[None, :]
    near = np.arange(ROWS, dtype=np.float64)[:, None] * freqs
    far = (np.arange(prompt_len // ROWS + 1, dtype=np.float64) * ROWS)[:, None] * freqs
    tables = (np.cos(near), np.sin(near) * sign, np.cos(far), np.sin(far) * sign)
    return [t.astype(np.float32) for t in tables]


def kernel(
    prompt, gain, w_query, w_key, w_value, q_gain, k_gain, table, ids, near_c, near_s, far_c, far_s, spread,
    out, dec,
    x, wq, wkv, tab, q, kbuf, vbuf, acc, top, es, er, eb, ec, eh, xs, qd, accd, topd, fsend, frecv,
    load_sem, wq_sem, ks, kr, vs, vr, e1s, e1r, e2s, e2r, e3s, e3r, qs, qr, fs, fr,
):
    ctx = lax.axis_index("ctx")
    tp = lax.axis_index("tp")
    chip = ctx // 2
    core = ctx % 2
    z = ctx // 4
    yh = chip % 2

    def remote(src, dst, send, recv, to_ctx, to_tp):
        return pltpu.make_async_remote_copy(
            src_ref=src, dst_ref=dst, send_sem=send, recv_sem=recv,
            device_id=(to_ctx, to_tp), device_id_type=MESH,
        )

    prompt_loads = []
    for n in range(4):
        rows = pl.ds(n * 128, 128)
        prompt_loads.append(pltpu.make_async_copy(prompt.at[rows], x.at[rows], load_sem.at[n]))
    key_load = pltpu.make_async_copy(w_key, wkv.at[:, pl.ds(0, HD)], load_sem.at[4])
    value_load = pltpu.make_async_copy(w_value, wkv.at[:, pl.ds(HD, HD)], load_sem.at[5])
    table_load = pltpu.make_async_copy(table, tab, load_sem.at[6])
    query_loads = []
    for n in range(2):
        cols = pl.ds((1 - n) * 512, 512)
        query_loads.append(pltpu.make_async_copy(w_query.at[:, cols], wq.at[:, cols], wq_sem.at[n]))
    for load in (*prompt_loads, key_load, value_load, query_loads[0], table_load, query_loads[1]):
        load.start()

    barrier = pltpu.get_barrier_semaphore()

    @pl.loop(1, NCTX)
    def _(i):
        pl.semaphore_signal(barrier, inc=1, device_id=((ctx + i) % NCTX, tp), device_id_type=MESH)

    @pl.loop(1, NTP)
    def _(i):
        pl.semaphore_signal(barrier, inc=1, device_id=(ctx, (tp + i) % NTP), device_id_type=MESH)

    def normed(rows_f32):
        mean_square = jnp.mean(rows_f32 * rows_f32, axis=-1, keepdims=True)
        return (rows_f32 * lax.rsqrt(mean_square + EPS) * gain[...]).astype(jnp.bfloat16)

    for n in range(4):
        prompt_loads[n].wait()

        @pl.loop(0, 8, unroll=2)
        def _(i):
            rows = pl.ds(pl.multiple_of(n * 128 + i * 16, 16), 16)
            x[rows, :] = normed(x[rows, :].astype(jnp.float32))

    def rotated(raw, head_gain, cosine, sine):
        mean_square = jnp.mean(raw * raw, axis=-1, keepdims=True)
        y = raw * lax.rsqrt(mean_square + EPS) * head_gain
        return (y * cosine + pltpu.roll(y, HD // 2, 1) * sine).astype(jnp.bfloat16)

    base_c, base_s = far_c[pl.ds(ctx, 1), :], far_s[pl.ds(ctx, 1), :]
    cosine = near_c[...] * base_c - near_s[...] * base_s
    sine = near_s[...] * base_c + near_c[...] * base_s

    key_load.wait()
    value_load.wait()
    kv = jnp.dot(x[...], wkv[...], preferred_element_type=jnp.float32)
    kbuf[ctx] = rotated(kv[:, :HD], k_gain[...], cosine, sine)
    vbuf[ctx] = kv[:, HD:].T.astype(jnp.bfloat16)

    pl.semaphore_wait(barrier, NCTX + NTP - 2)

    def block(zz, yy, cc):
        return zz * 4 + yy * 2 + cc

    zp, zm, z2 = (z + 1) % 4, (z + 3) % 4, (z + 2) % 4
    sib = block(z, yh, 1 - core)
    up, down, across = block(zp, yh, core), block(zm, yh, core), block(z, 1 - yh, core)
    sent = []

    def send(kind, b, to):
        if kind == "k":
            n = sum(1 for s in sent if s[0] == "k")
            copy = remote(kbuf.at[b], kbuf.at[b], ks.at[n], kr.at[b], to, tp)
        else:
            n = sum(1 for s in sent if s[0] == "v")
            copy = remote(vbuf.at[b], vbuf.at[b], vs.at[n], vr.at[b], to, tp)
        copy.start()
        sent.append((kind, copy))

    def arrived(kind, b):
        if kind == "k":
            remote(kbuf.at[b], kbuf.at[b], ks.at[0], kr.at[b], sib, tp).wait_recv()
        else:
            remote(vbuf.at[b], vbuf.at[b], vs.at[0], vr.at[b], sib, tp).wait_recv()

    def hop_own():
        for to in (across, up, down, sib):
            send("k", ctx, to)
            send("v", ctx, to)

    def hop_ring(yy):
        left, right = block(zm, yy, core), block(zp, yy, core)
        arrived("k", left)
        send("k", left, up)
        arrived("v", right)
        send("v", right, down)
        arrived("v", left)
        arrived("k", right)
        for b in (left, right):
            send("k", b, sib)
            send("v", b, sib)

    def hop_across():
        b = across
        arrived("k", b)
        arrived("v", b)
        for to in (up, down, sib):
            send("k", b, to)
            send("v", b, to)

    def hop_far(yy):
        b = block(z2, yy, core)
        arrived("k", b)
        arrived("v", b)
        send("k", b, sib)
        send("v", b, sib)

    hop_own()

    table_load.wait()
    first_row = (ctx * NTP + tp) * VROWS
    lanes = lax.broadcasted_iota(jnp.int32, (64, VROWS), 1)
    picks = (ids[...] - first_row == lanes).astype(jnp.bfloat16)
    for n in range(NTP):
        cols = slice(n * PIECE, (n + 1) * PIECE)
        es[n] = jnp.dot(picks, tab[:, cols], preferred_element_type=jnp.float32).astype(jnp.bfloat16)
    er[tp] = es[tp]

    @pl.loop(1, NTP)
    def _(i):
        to = (tp + i) % NTP
        remote(es.at[to], er.at[tp], e1s.at[i], e1r.at[tp], ctx, to).start()

    light = chip < 4
    moved = jnp.where(light, 4 - chip, chip - 3)
    partner = block(3 - z, 1 - yh, core)
    kept = jnp.where(light, HEADS, HEADS - moved)

    def project_queries(first):
        raw = jnp.dot(x[...], wq[:, first * HD:(first + 4) * HD], preferred_element_type=jnp.float32)
        for h in range(4):
            q[first + h] = rotated(raw[:, h * HD:(h + 1) * HD], q_gain[...], cosine, sine)

    query_loads[0].wait()
    project_queries(4)

    def query_copy(f):
        return remote(q.at[kept + f], q.at[HEADS + f], qs.at[f], qr.at[f], partner, tp)

    @pl.when(jnp.logical_not(light))
    def _():
        @pl.loop(0, moved)
        def _(f):
            query_copy(f).start()

    @pl.loop(1, NTP)
    def _(i):
        frm = (tp + i) % NTP
        remote(es.at[frm], er.at[frm], e1s.at[i], e1r.at[frm], ctx, frm).wait_recv()

    piece = er[0].astype(jnp.float32)
    for n in range(1, NTP):
        piece = piece + er[n].astype(jnp.float32)
    piece = jnp.dot(spread[...], piece.astype(jnp.bfloat16), preferred_element_type=jnp.float32)
    eb[...] = piece.astype(jnp.bfloat16).reshape(NCTX, 16, PIECE)
    ec[ctx] = eb[ctx]

    @pl.loop(1, NCTX)
    def _(i):
        to = (ctx + i) % NCTX
        remote(eb.at[to], ec.at[ctx], e2s.at[i], e2r.at[ctx], to, tp).start()

    query_loads[1].wait()
    project_queries(0)
    hop_ring(yh)

    @pl.loop(1, NCTX)
    def _(i):
        frm = (ctx + i) % NCTX
        remote(eb.at[frm], ec.at[frm], e2s.at[i], e2r.at[frm], frm, tp).wait_recv()

    piece = ec[0].astype(jnp.float32)
    for n in range(1, NCTX):
        piece = piece + ec[n].astype(jnp.float32)
    eh[tp] = piece.astype(jnp.bfloat16)

    def piece_copy(i, to, frm):
        return remote(eh.at[frm], eh.at[frm], e3s.at[i], e3r.at[frm], ctx, to)

    @pl.loop(1, NTP)
    def _(i):
        piece_copy(i, (tp + i) % NTP, tp).start()

    ones = jnp.ones((16, PAIR), jnp.bfloat16)

    def pair_keys(j):
        return kbuf[pl.ds(2 * j, 2)].reshape(PAIR, HD)

    def pair_values(j):
        values = jnp.concatenate([vbuf[2 * j], vbuf[2 * j + 1]], axis=1)
        return jnp.concatenate([values, ones], axis=0)

    def scores(keys, queries):
        return lax.dot_general(keys, queries, (((1,), (1,)), ((), ())), preferred_element_type=jnp.float32)

    def pipeline(units, first, second, third):
        held, mixed = {}, {}
        count = len(units)
        for t in range(count + 2):
            if t < count:
                held[t] = first(units[t])
            if 0 <= t - 2:
                third(units[t - 2], mixed.pop(t - 2))
            if 0 <= t - 1 < count:
                mixed[t - 1] = second(units[t - 1], held.pop(t - 1))

    def unit_scores(unit):
        j, source, _ = unit
        return scores(pair_keys(j), q[source])

    arrived("k", sib)
    arrived("v", sib)
    later = lax.broadcasted_iota(jnp.int32, (PAIR, ROWS), 0) - lax.broadcasted_iota(jnp.int32, (PAIR, ROWS), 1)

    def open_weights(unit, s):
        s = jnp.where(later <= core * ROWS, s, LOW)
        peak = jnp.max(s, axis=0, keepdims=True) * SCALE
        top[unit[2], :1, :] = peak
        return jnp.exp2(s * SCALE - peak).astype(jnp.bfloat16)

    def open_mix(unit, weights):
        acc[unit[2]] = jnp.dot(pair_values(unit[0]), weights, preferred_element_type=jnp.float32)

    def next_weights(unit, s):
        before = top[unit[2], :1, :]
        peak = jnp.maximum(before, jnp.max(s, axis=0, keepdims=True) * SCALE)
        top[unit[2], :1, :] = peak
        return jnp.exp2(s * SCALE - peak).astype(jnp.bfloat16), jnp.exp2(before - peak)

    def next_mix(unit, weights):
        w, factor = weights
        slot = unit[2]
        acc[slot] = acc[slot] * factor + jnp.dot(pair_values(unit[0]), w, preferred_element_type=jnp.float32)

    def open_heads(begin, count, j):
        @pl.loop(0, (count + 3) // 4)
        def _(g):
            units = []
            for n in range(4):
                h = g * 4 + n
                use = h < count
                units.append((j, jnp.where(use, begin + h, 0), jnp.where(use, begin + h, SPARE)))
            pipeline(units, unit_scores, open_weights, open_mix)

    open_heads(0, kept, chip)
    hop_across()
    hop_far(yh)

    @pl.loop(1, NTP)
    def _(i):
        frm = (tp + i) % NTP
        piece_copy(i, frm, frm).wait_recv()

    hidden = jnp.concatenate([eh[n] for n in range(NTP)], axis=1).astype(jnp.float32)
    xs[...] = normed(hidden)
    step_c, step_s = far_c[NCTX:NCTX + 1, :], far_s[NCTX:NCTX + 1, :]
    dec_c = near_c[:16, :] * step_c - near_s[:16, :] * step_s
    dec_s = near_s[:16, :] * step_c + near_c[:16, :] * step_s
    step_kv = jnp.dot(xs[...], wkv[...], preferred_element_type=jnp.float32)
    step_k = rotated(step_kv[:, :HD], k_gain[...], dec_c, dec_s)
    step_v = step_kv[:, HD:].astype(jnp.bfloat16)
    for g in range(2):
        raw = jnp.dot(xs[...], wq[:, g * 512:(g + 1) * 512], preferred_element_type=jnp.float32)
        for h in range(4):
            rows = slice((g * 4 + h) * 16, (g * 4 + h + 1) * 16)
            qd[rows, :] = rotated(raw[:, h * HD:(h + 1) * HD], q_gain[...], dec_c, dec_s)

    own = scores(step_k, qd[...])
    step = lax.broadcasted_iota(jnp.int32, (16, HD), 1) % 16
    own = jnp.where(lax.broadcasted_iota(jnp.int32, (16, HD), 0) <= step, own, LOW)
    peak = jnp.max(own, axis=0, keepdims=True) * SCALE
    weights = jnp.exp2(own * SCALE - peak).astype(jnp.bfloat16)
    topd[:1, :] = peak
    step_values = jnp.concatenate([step_v, jnp.ones((16, 16), jnp.bfloat16)], axis=1)
    accd[...] = lax.dot_general(
        step_values, weights, (((0,), (0,)), ((), ())), preferred_element_type=jnp.float32
    )

    hop_ring(1 - yh)
    hop_far(1 - yh)
    for zz, yy in ((zm, yh), (zp, yh), (z2, yh), (z, 1 - yh), (zm, 1 - yh), (zp, 1 - yh), (z2, 1 - yh)):
        arrived("k", block(zz, yy, 1 - core))
        arrived("v", block(zz, yy, 1 - core))

    @pl.when(light)
    def _():
        @pl.loop(0, moved)
        def _(f):
            query_copy(f).wait_recv()

        open_heads(HEADS, moved, 7 - chip)

    own_units = kept * chip
    all_units = jnp.where(light, own_units + moved * (7 - chip), own_units)
    top[SPARE] = jnp.zeros((8, ROWS), jnp.float32)

    @pl.loop(0, (all_units + GROUP - 1) // GROUP)
    def _(g):
        units = []
        for n in range(GROUP):
            u = g * GROUP + n
            rest = u - own_units
            mine = rest < 0
            use = u < all_units
            j = jnp.where(mine, u // kept, rest // moved)
            slot = jnp.where(mine, u % kept, HEADS + rest % moved)
            units.append((jnp.where(use, j, 0), jnp.where(use, slot, 0), jnp.where(use, slot, SPARE)))
        pipeline(units, unit_scores, next_weights, next_mix)

    def finished(slot):
        mix = acc[slot]
        return (mix[:HD] * (1.0 / mix[HD:HD + 1])).T.astype(jnp.bfloat16)

    def result_copy(f):
        return remote(fsend.at[f], frecv.at[f], fs.at[f], fr.at[f], partner, tp)

    @pl.when(light)
    def _():
        @pl.loop(0, moved)
        def _(f):
            fsend[f] = finished(HEADS + f)
            result_copy(f).start()

    def step_weights(j, s):
        before = topd[:1, :]
        peak = jnp.maximum(before, jnp.max(s, axis=0, keepdims=True) * SCALE)
        topd[:1, :] = peak
        return jnp.exp2(s * SCALE - peak).astype(jnp.bfloat16), jnp.exp2(before - peak)

    def step_mix(j, weights):
        w, factor = weights
        accd[...] = accd[...] * factor + jnp.dot(pair_values(j), w, preferred_element_type=jnp.float32)

    @pl.loop(0, 2)
    def _(g):
        pipeline([g * 4 + n for n in range(4)], lambda j: scores(pair_keys(j), qd[...]), step_weights, step_mix)

    mix = accd[...]
    steps = (mix[:HD] * (1.0 / mix[HD:HD + 1])).T.astype(jnp.bfloat16)
    for h in range(HEADS):
        dec[:, h * HD:(h + 1) * HD] = steps[h * 16:(h + 1) * 16, :]

    @pl.loop(0, kept)
    def _(h):
        out[:, pl.ds(pl.multiple_of(h * HD, HD), HD)] = finished(h)

    @pl.when(jnp.logical_not(light))
    def _():
        @pl.loop(0, moved)
        def _(f):
            result_copy(f).wait_recv()
            out[:, pl.ds(pl.multiple_of((kept + f) * HD, HD), HD)] = frecv[f]
            query_copy(f).wait_send()

    @pl.when(light)
    def _():
        @pl.loop(0, moved)
        def _(f):
            result_copy(f).wait_send()

    for _, copy in sent:
        copy.wait_send()

    @pl.loop(1, NTP)
    def _(i):
        to = (tp + i) % NTP
        remote(es.at[to], er.at[tp], e1s.at[i], e1r.at[tp], ctx, to).wait_send()
        piece_copy(i, to, tp).wait_send()

    @pl.loop(1, NCTX)
    def _(i):
        to = (ctx + i) % NCTX
        remote(eb.at[to], ec.at[ctx], e2s.at[i], e2r.at[ctx], to, tp).wait_send()


def body(prompt, norm_gain, w_query, w_key, w_value, query_gain, key_gain, table, sampled):
    near_c, near_s, far_c, far_s = rope_tables(NCTX * ROWS)
    spread = np.zeros((NCTX * 16, 64), np.float32)
    for s in range(NCTX):
        for j in range(4):
            spread[s * 16 + j, s * 4 + j] = 1.0
    hbm = pl.BlockSpec(memory_space=pl.ANY)
    vmem = pl.BlockSpec(memory_space=pltpu.VMEM)
    bf, f32 = jnp.bfloat16, jnp.float32
    dma = pltpu.SemaphoreType.DMA
    out, dec = pl.pallas_call(
        kernel,
        out_shape=(
            jax.ShapeDtypeStruct((ROWS, HEADS * HD), bf),
            jax.ShapeDtypeStruct((16, HEADS * HD), bf),
        ),
        in_specs=[hbm, vmem, hbm, hbm, hbm, vmem, vmem, hbm] + [vmem] * 6,
        out_specs=(vmem, vmem),
        scratch_shapes=[
            pltpu.VMEM((ROWS, D), bf),
            pltpu.VMEM((D, HEADS * HD), bf),
            pltpu.VMEM((D, 2 * HD), bf),
            pltpu.VMEM((VROWS, D), bf),
            pltpu.VMEM((12, ROWS, HD), bf),
            pltpu.VMEM((NCTX, ROWS, HD), bf),
            pltpu.VMEM((NCTX, HD, ROWS), bf),
            pltpu.VMEM((SPARE + 1, ACC, ROWS), f32),
            pltpu.VMEM((SPARE + 1, 8, ROWS), f32),
            pltpu.VMEM((NTP, 64, PIECE), bf),
            pltpu.VMEM((NTP, 64, PIECE), bf),
            pltpu.VMEM((NCTX, 16, PIECE), bf),
            pltpu.VMEM((NCTX, 16, PIECE), bf),
            pltpu.VMEM((NTP, 16, PIECE), bf),
            pltpu.VMEM((16, D), bf),
            pltpu.VMEM((HD, HD), bf),
            pltpu.VMEM((ACC, HD), f32),
            pltpu.VMEM((8, HD), f32),
            pltpu.VMEM((4, ROWS, HD), bf),
            pltpu.VMEM((4, ROWS, HD), bf),
            dma((7,)), dma((2,)),
            dma((15,)), dma((NCTX,)), dma((15,)), dma((NCTX,)),
            dma((NTP,)), dma((NTP,)), dma((NCTX,)), dma((NCTX,)), dma((NTP,)), dma((NTP,)),
            dma((4,)), dma((4,)), dma((4,)), dma((4,)),
        ],
        compiler_params=pltpu.CompilerParams(
            collective_id=0, has_side_effects=True, vmem_limit_bytes=62 * 2**20
        ),
    )(
        prompt, norm_gain[None, :], w_query, w_key, w_value, query_gain[None, :], key_gain[None, :], table,
        sampled.reshape(64, 1), near_c, near_s, far_c, far_s, spread.astype(jnp.bfloat16),
    )
    return out, dec[None, :4]


def solution(mesh):
    in_specs = (
        P("ctx", None),
        P(),
        P(None, "tp"),
        P(None, "tp"),
        P(None, "tp"),
        P(),
        P(),
        P(("ctx", "tp"), None),
        P(),
    )
    out_specs = (P("ctx", "tp"), P("ctx", None, "tp"))
    return jax.shard_map(body, mesh=mesh, in_specs=in_specs, out_specs=out_specs, check_vma=False)
```

time: 378 us -> 111 us (0.29)
  the two profiles are of different devices: /device:TPU:121 before, /device:TPU:1 now
where the time goes in v1:
time: 111 us
  Pallas kernels  105 us (95%)
  local copies, waits for them, and re-layouts  5.03 us (5%)
    pallas_call x1, Pallas kernels, body(): pl.pallas_call(kernel, out_shape=(jax.ShapeDtypeStruct((ROWS, HEADS * HD)...  105 us
    unnamed x2, local copies, waits for them, and re-layouts  3.02 us

profile of v1, /device:TPU:1, one launch (start us, length us, event | category | flops | bytes accessed | tf_op | source)
XLA Modules:
  0.0 110.9 jit_solution(6886255843760264809)
XLA Ops:
  0.6 0.8 copy.18
  1.4 0.7 reshape.8.ids
  2.1 105.2 %shard_map.149 = (bf16[512,1024]{1,0:T(8,128)(2,1)}, bf16[16,1024]{1,0:T(8,128)(2,1)}) custom-call(bf16[512,5120]{1,0:T(8,128)(2,1)} %prompt.1, f32[1,5120]{1,0:T(1,128)} %bitcast.5, bf16[5120,1024]{1,0:T(8,128)(2,1)} %w_query.1, bf16[5120,128]{1,0:T(8,128)(2,1)} %w_key.1, bf16[5120,128]{1,0:T(8,128)(2,1)} %w_value.1, f32[1,128]{1,0:T(1,128)} %bitcast.6, ...), custom_call_target="tpu_custom_call" | custom-call | tf_op jit(solution)/shard_map/pallas_call | solution.py:447
  107.3 1.3 %slice_bitcast_fusion = bf16[1,4,1024]{2,1,0:T(4,128)(2,1)} fusion(bf16[16,1024]{1,0:T(8,128)(2,1)} %get-tuple-element.5), kind=kLoop, calls=%fused_computation | loop fusion | bytes 16384 | tf_op jit(solution)/shard_map/broadcast_in_dim | solution.py:488
  108.6 2.3 %copy.21 = bf16[512,1024]{1,0:T(8,128)(2,1)} copy(bf16[512,1024]{1,0:T(8,128)(2,1)} %get-tuple-element.8) | data formatting | bytes 2097152

commit v2 on v1

--- a/solution.py
+++ b/solution.py
@@ -22,8 +22,9 @@
 PIECE = D // NTP
 SCALE = HD ** (-0.5) * 1.4426950408889634
 LOW = -1e30
-GROUP = 10
-SPARE = 12
+GROUP = 5
+SPARE = 11
+TAKEN = (3, 3, 2, 1)
 ACC = HD + 16
 
 
@@ -36,6 +37,27 @@
     far = (np.arange(prompt_len // ROWS + 1, dtype=np.float64) * ROWS)[:, None] * freqs
     tables = (np.cos(near), np.sin(near) * sign, np.cos(far), np.sin(far) * sign)
     return [t.astype(np.float32) for t in tables]
+
+
+def pair_lists(chip):
+    zz, yy = chip // 2, chip % 2
+    at = lambda dz, y: (zz + dz) % 4 * 2 + y
+    soon = [at(0, 1 - yy), at(3, yy), at(1, yy), at(2, yy)]
+    late = [at(3, 1 - yy), at(1, 1 - yy), at(2, 1 - yy)]
+    cut = lambda pairs, limit: [j for j in pairs if j < limit]
+    lists = [cut(soon, chip), cut(late, chip)]
+    lists += [cut([chip] + soon, 7 - chip), cut(late, 7 - chip)] if chip < 4 else [[], []]
+    return [(len(pairs), sum(j << (3 * k) for k, j in enumerate(pairs))) for pairs in lists]
+
+
+PAIR_LISTS = [pair_lists(chip) for chip in range(8)]
+
+
+def pick(index, values):
+    result = index * 0 + values[-1]
+    for n, value in enumerate(values[:-1]):
+        result = result + (index == n).astype(jnp.int32) * (value - values[-1])
+    return result
 
 
 def kernel(
@@ -68,7 +90,7 @@
     for n in range(2):
         cols = pl.ds((1 - n) * 512, 512)
         query_loads.append(pltpu.make_async_copy(w_query.at[:, cols], wq.at[:, cols], wq_sem.at[n]))
-    for load in (*prompt_loads, key_load, value_load, query_loads[0], table_load, query_loads[1]):
+    for load in (*prompt_loads, key_load, value_load):
         load.start()
 
     barrier = pltpu.get_barrier_semaphore()
@@ -92,6 +114,11 @@
         def _(i):
             rows = pl.ds(pl.multiple_of(n * 128 + i * 16, 16), 16)
             x[rows, :] = normed(x[rows, :].astype(jnp.float32))
+
+        if n == 2:
+            query_loads[0].start()
+    query_loads[1].start()
+    table_load.start()
 
     def rotated(raw, head_gain, cosine, sine):
         mean_square = jnp.mean(raw * raw, axis=-1, keepdims=True)
@@ -116,31 +143,33 @@
     zp, zm, z2 = (z + 1) % 4, (z + 3) % 4, (z + 2) % 4
     sib = block(z, yh, 1 - core)
     up, down, across = block(zp, yh, core), block(zm, yh, core), block(z, 1 - yh, core)
+    late_left, late_right, late_far = (block(n, 1 - yh, core) for n in (zm, zp, z2))
     sent = []
 
+    def block_copy(kind, n, b, to):
+        buffer, out_sem, in_sem = (kbuf, ks, kr) if kind == "k" else (vbuf, vs, vr)
+        return remote(buffer.at[b], buffer.at[b], out_sem.at[n], in_sem.at[b], to, tp)
+
     def send(kind, b, to):
-        if kind == "k":
-            n = sum(1 for s in sent if s[0] == "k")
-            copy = remote(kbuf.at[b], kbuf.at[b], ks.at[n], kr.at[b], to, tp)
-        else:
-            n = sum(1 for s in sent if s[0] == "v")
-            copy = remote(vbuf.at[b], vbuf.at[b], vs.at[n], vr.at[b], to, tp)
-        copy.start()
-        sent.append((kind, copy))
+        n = sum(1 for item in sent if item[0] == kind)
+        block_copy(kind, n, b, to).start()
+        sent.append((kind, n, b, to))
 
     def arrived(kind, b):
-        if kind == "k":
-            remote(kbuf.at[b], kbuf.at[b], ks.at[0], kr.at[b], sib, tp).wait_recv()
-        else:
-            remote(vbuf.at[b], vbuf.at[b], vs.at[0], vr.at[b], sib, tp).wait_recv()
+        block_copy(kind, 0, b, sib).wait_recv()
 
     def hop_own():
-        for to in (across, up, down, sib):
-            send("k", ctx, to)
-            send("v", ctx, to)
-
-    def hop_ring(yy):
-        left, right = block(zm, yy, core), block(zp, yy, core)
+        send("k", ctx, up)
+        send("v", ctx, down)
+        send("k", ctx, across)
+        send("v", ctx, across)
+        send("v", ctx, up)
+        send("k", ctx, down)
+        send("k", ctx, sib)
+        send("v", ctx, sib)
+
+    def hop_ring():
+        left, right = block(zm, yh, core), block(zp, yh, core)
         arrived("k", left)
         send("k", left, up)
         arrived("v", right)
@@ -152,38 +181,27 @@
             send("v", b, sib)
 
     def hop_across():
-        b = across
+        arrived("k", across)
+        arrived("v", across)
+        for to in (up, down, sib):
+            send("k", across, to)
+            send("v", across, to)
+
+    def hop_last(b, *more):
         arrived("k", b)
         arrived("v", b)
-        for to in (up, down, sib):
+        for to in (*more, sib):
             send("k", b, to)
             send("v", b, to)
 
-    def hop_far(yy):
-        b = block(z2, yy, core)
-        arrived("k", b)
-        arrived("v", b)
-        send("k", b, sib)
-        send("v", b, sib)
+    def from_sib(zz, yy):
+        arrived("k", block(zz, yy, 1 - core))
+        arrived("v", block(zz, yy, 1 - core))
 
     hop_own()
 
-    table_load.wait()
-    first_row = (ctx * NTP + tp) * VROWS
-    lanes = lax.broadcasted_iota(jnp.int32, (64, VROWS), 1)
-    picks = (ids[...] - first_row == lanes).astype(jnp.bfloat16)
-    for n in range(NTP):
-        cols = slice(n * PIECE, (n + 1) * PIECE)
-        es[n] = jnp.dot(picks, tab[:, cols], preferred_element_type=jnp.float32).astype(jnp.bfloat16)
-    er[tp] = es[tp]
-
-    @pl.loop(1, NTP)
-    def _(i):
-        to = (tp + i) % NTP
-        remote(es.at[to], er.at[tp], e1s.at[i], e1r.at[tp], ctx, to).start()
-
     light = chip < 4
-    moved = jnp.where(light, 4 - chip, chip - 3)
+    moved = pick(chip, TAKEN + TAKEN[::-1])
     partner = block(3 - z, 1 - yh, core)
     kept = jnp.where(light, HEADS, HEADS - moved)
 
@@ -204,43 +222,26 @@
         def _(f):
             query_copy(f).start()
 
-    @pl.loop(1, NTP)
-    def _(i):
-        frm = (tp + i) % NTP
-        remote(es.at[frm], er.at[frm], e1s.at[i], e1r.at[frm], ctx, frm).wait_recv()
-
-    piece = er[0].astype(jnp.float32)
-    for n in range(1, NTP):
-        piece = piece + er[n].astype(jnp.float32)
-    piece = jnp.dot(spread[...], piece.astype(jnp.bfloat16), preferred_element_type=jnp.float32)
-    eb[...] = piece.astype(jnp.bfloat16).reshape(NCTX, 16, PIECE)
-    ec[ctx] = eb[ctx]
-
-    @pl.loop(1, NCTX)
-    def _(i):
-        to = (ctx + i) % NCTX
-        remote(eb.at[to], ec.at[ctx], e2s.at[i], e2r.at[ctx], to, tp).start()
-
     query_loads[1].wait()
     project_queries(0)
-    hop_ring(yh)
-
-    @pl.loop(1, NCTX)
-    def _(i):
-        frm = (ctx + i) % NCTX
-        remote(eb.at[frm], ec.at[frm], e2s.at[i], e2r.at[frm], frm, tp).wait_recv()
-
-    piece = ec[0].astype(jnp.float32)
-    for n in range(1, NCTX):
-        piece = piece + ec[n].astype(jnp.float32)
-    eh[tp] = piece.astype(jnp.bfloat16)
-
-    def piece_copy(i, to, frm):
-        return remote(eh.at[frm], eh.at[frm], e3s.at[i], e3r.at[frm], ctx, to)
+    table_load.wait()
+    first_row = (ctx * NTP + tp) * VROWS
+    lanes = (lax.broadcasted_iota(jnp.int32, (16, VROWS), 1) + first_row).astype(jnp.float32)
+    diagonal = lax.broadcasted_iota(jnp.int32, (16, 16), 0) == lax.broadcasted_iota(jnp.int32, (16, 16), 1)
+    picks = []
+    for j in range(4):
+        wanted = jnp.where(diagonal, ids[j:j + 1, :].astype(jnp.float32), 0.0)
+        picks.append((jnp.sum(wanted, axis=1, keepdims=True) == lanes).astype(jnp.float32))
+    picks = jnp.concatenate(picks, axis=0).astype(jnp.bfloat16)
+    for n in range(NTP):
+        cols = slice(n * PIECE, (n + 1) * PIECE)
+        es[n] = jnp.dot(picks, tab[:, cols], preferred_element_type=jnp.float32).astype(jnp.bfloat16)
+    er[tp] = es[tp]
 
     @pl.loop(1, NTP)
     def _(i):
-        piece_copy(i, (tp + i) % NTP, tp).start()
+        to = (tp + i) % NTP
+        remote(es.at[to], er.at[tp], e1s.at[i], e1r.at[tp], ctx, to).start()
 
     ones = jnp.ones((16, PAIR), jnp.bfloat16)
 
@@ -288,24 +289,147 @@
         top[unit[2], :1, :] = peak
         return jnp.exp2(s * SCALE - peak).astype(jnp.bfloat16), jnp.exp2(before - peak)
 
+    def last_weights(unit, s):
+        return next_weights(unit, jnp.where(later <= core * ROWS, s, LOW))
+
     def next_mix(unit, weights):
         w, factor = weights
         slot = unit[2]
         acc[slot] = acc[slot] * factor + jnp.dot(pair_values(unit[0]), w, preferred_element_type=jnp.float32)
 
-    def open_heads(begin, count, j):
-        @pl.loop(0, (count + 3) // 4)
-        def _(g):
+    def open_heads(begin, count):
+        units = []
+        for n in range(4):
+            use = n < count
+            units.append((chip, jnp.where(use, begin + n, 0), jnp.where(use, begin + n, SPARE)))
+        pipeline(units, unit_scores, open_weights, open_mix)
+
+    open_heads(chip * 0, chip * 0 + 4)
+    hop_ring()
+    open_heads(chip * 0 + 4, kept - 4)
+    hop_across()
+    @pl.loop(1, NTP)
+    def _(i):
+        frm = (tp + i) % NTP
+        remote(es.at[frm], er.at[frm], e1s.at[i], e1r.at[frm], ctx, frm).wait_recv()
+
+    piece = er[0].astype(jnp.float32)
+    for n in range(1, NTP):
+        piece = piece + er[n].astype(jnp.float32)
+    piece = jnp.dot(spread[...], piece.astype(jnp.bfloat16), preferred_element_type=jnp.float32)
+    eb[...] = piece.astype(jnp.bfloat16).reshape(NCTX, 16, PIECE)
+    ec[ctx] = eb[ctx]
+
+    @pl.loop(1, NCTX)
+    def _(i):
+        to = (ctx + i) % NCTX
+        remote(eb.at[to], ec.at[ctx], e2s.at[i], e2r.at[ctx], to, tp).start()
+
+    hop_last(block(z2, yh, core), across)
+    for zz, yy in ((z, 1 - yh), (zm, yh), (zp, yh), (z2, yh)):
+        from_sib(zz, yy)
+
+    @pl.when(light)
+    def _():
+        @pl.loop(0, moved)
+        def _(f):
+            query_copy(f).wait_recv()
+            acc[HEADS + f] = jnp.zeros((ACC, ROWS), jnp.float32)
+            top[HEADS + f] = jnp.full((8, ROWS), LOW, jnp.float32)
+
+    acc[SPARE] = jnp.zeros((ACC, ROWS), jnp.float32)
+    top[SPARE] = jnp.zeros((8, ROWS), jnp.float32)
+
+    def settle(turn, k, h, sizes):
+        for n in range(2):
+            end = (turn == n) & (k >= sizes[n])
+            turn = jnp.where(end, n + 1, turn)
+            k = jnp.where(end, 0, k)
+        return turn, k, h
+
+    def run_pairs(own_list, other_list, own_first, between=None):
+        tables = [[PAIR_LISTS[c][n] for c in range(8)] for n in (own_list, other_list)]
+        sizes = [pick(chip, [entry[0] for entry in t]) for t in tables]
+        codes = [pick(chip, [entry[1] for entry in t]) for t in tables]
+        widths, bases = [kept, moved], [chip * 0, chip * 0 + HEADS]
+        if not own_first:
+            for items in (sizes, codes, widths, bases):
+                items.reverse()
+        total = sizes[0] * widths[0] + sizes[1] * widths[1]
+
+        def step(g, state):
+            if between is not None:
+                between(g)
             units = []
-            for n in range(4):
-                h = g * 4 + n
-                use = h < count
-                units.append((j, jnp.where(use, begin + h, 0), jnp.where(use, begin + h, SPARE)))
-            pipeline(units, unit_scores, open_weights, open_mix)
-
-    open_heads(0, kept, chip)
-    hop_across()
-    hop_far(yh)
+            for n in range(GROUP):
+                turn, k, h = state
+                first = turn == 0
+                use = turn < 2
+                j = lax.shift_right_logical(jnp.where(first, codes[0], codes[1]), 3 * k) % 8
+                slot = jnp.where(first, bases[0], bases[1]) + h
+                units.append((jnp.where(use, j, chip), jnp.where(use, slot, 0), jnp.where(use, slot, SPARE)))
+                h = h + 1
+                wrap = h >= jnp.where(first, widths[0], widths[1])
+                state = settle(turn, k + wrap.astype(jnp.int32), jnp.where(wrap, 0, h), sizes)
+            pipeline(units, unit_scores, next_weights, next_mix)
+            return state
+
+        start = settle(chip * 0, chip * 0, chip * 0, sizes)
+        lax.fori_loop(0, (total + GROUP - 1) // GROUP, step, start)
+
+    def hops_between(g):
+        @pl.when(g == 1)
+        def _():
+            hop_last(late_left)
+            hop_last(late_right)
+
+        @pl.when(g == 2)
+        def _():
+            hop_last(late_far)
+
+    run_pairs(0, 2, True, hops_between)
+
+    @pl.loop(1, NCTX)
+    def _(i):
+        frm = (ctx + i) % NCTX
+        remote(eb.at[frm], ec.at[frm], e2s.at[i], e2r.at[frm], frm, tp).wait_recv()
+
+    piece = ec[0].astype(jnp.float32)
+    for n in range(1, NCTX):
+        piece = piece + ec[n].astype(jnp.float32)
+    eh[tp] = piece.astype(jnp.bfloat16)
+
+    def piece_copy(i, to, frm):
+        return remote(eh.at[frm], eh.at[frm], e3s.at[i], e3r.at[frm], ctx, to)
+
+    @pl.loop(1, NTP)
+    def _(i):
+        piece_copy(i, (tp + i) % NTP, tp).start()
+
+    for zz in (zm, zp, z2):
+        from_sib(zz, 1 - yh)
+    run_pairs(1, 3, False)
+
+    def finished(slot):
+        mix = acc[slot]
+        return (mix[:HD] * (1.0 / mix[HD:HD + 1])).T.astype(jnp.bfloat16)
+
+    def result_copy(f):
+        return remote(fsend.at[f], frecv.at[f], fs.at[f], fr.at[f], partner, tp)
+
+    @pl.when(light)
+    def _():
+        units = []
+        for f in range(3):
+            use = f < moved
+            slot = HEADS + f + 0 * chip
+            units.append((7 - chip, jnp.where(use, slot, 0), jnp.where(use, slot, SPARE)))
+        pipeline(units, unit_scores, last_weights, next_mix)
+
+        @pl.loop(0, moved)
+        def _(f):
+            fsend[f] = finished(HEADS + f)
+            result_copy(f).start()
 
     @pl.loop(1, NTP)
     def _(i):
@@ -337,51 +461,6 @@
         step_values, weights, (((0,), (0,)), ((), ())), preferred_element_type=jnp.float32
     )
 
-    hop_ring(1 - yh)
-    hop_far(1 - yh)
-    for zz, yy in ((zm, yh), (zp, yh), (z2, yh), (z, 1 - yh), (zm, 1 - yh), (zp, 1 - yh), (z2, 1 - yh)):
-        arrived("k", block(zz, yy, 1 - core))
-        arrived("v", block(zz, yy, 1 - core))
-
-    @pl.when(light)
-    def _():
-        @pl.loop(0, moved)
-        def _(f):
-            query_copy(f).wait_recv()
-
-        open_heads(HEADS, moved, 7 - chip)
-
-    own_units = kept * chip
-    all_units = jnp.where(light, own_units + moved * (7 - chip), own_units)
-    top[SPARE] = jnp.zeros((8, ROWS), jnp.float32)
-
-    @pl.loop(0, (all_units + GROUP - 1) // GROUP)
-    def _(g):
-        units = []
-        for n in range(GROUP):
-            u = g * GROUP + n
-            rest = u - own_units
-            mine = rest < 0
-            use = u < all_units
-            j = jnp.where(mine, u // kept, rest // moved)
-            slot = jnp.where(mine, u % kept, HEADS + rest % moved)
-            units.append((jnp.where(use, j, 0), jnp.where(use, slot, 0), jnp.where(use, slot, SPARE)))
-        pipeline(units, unit_scores, next_weights, next_mix)
-
-    def finished(slot):
-        mix = acc[slot]
-        return (mix[:HD] * (1.0 / mix[HD:HD + 1])).T.astype(jnp.bfloat16)
-
-    def result_copy(f):
-        return remote(fsend.at[f], frecv.at[f], fs.at[f], fr.at[f], partner, tp)
-
-    @pl.when(light)
-    def _():
-        @pl.loop(0, moved)
-        def _(f):
-            fsend[f] = finished(HEADS + f)
-            result_copy(f).start()
-
     def step_weights(j, s):
         before = topd[:1, :]
         peak = jnp.maximum(before, jnp.max(s, axis=0, keepdims=True) * SCALE)
@@ -419,8 +498,8 @@
         def _(f):
             result_copy(f).wait_send()
 
-    for _, copy in sent:
-        copy.wait_send()
+    for item in sent:
+        block_copy(*item).wait_send()
 
     @pl.loop(1, NTP)
     def _(i):
@@ -439,7 +518,7 @@
     spread = np.zeros((NCTX * 16, 64), np.float32)
     for s in range(NCTX):
         for j in range(4):
-            spread[s * 16 + j, s * 4 + j] = 1.0
+            spread[s * 16 + j, j * 16 + s] = 1.0
     hbm = pl.BlockSpec(memory_space=pl.ANY)
     vmem = pl.BlockSpec(memory_space=pltpu.VMEM)
     bf, f32 = jnp.bfloat16, jnp.float32
@@ -474,7 +553,7 @@
             pltpu.VMEM((4, ROWS, HD), bf),
             pltpu.VMEM((4, ROWS, HD), bf),
             dma((7,)), dma((2,)),
-            dma((15,)), dma((NCTX,)), dma((15,)), dma((NCTX,)),
+            dma((16,)), dma((NCTX,)), dma((16,)), dma((NCTX,)),
             dma((NTP,)), dma((NTP,)), dma((NCTX,)), dma((NCTX,)), dma((NTP,)), dma((NTP,)),
             dma((4,)), dma((4,)), dma((4,)), dma((4,)),
         ],
@@ -483,7 +562,7 @@
         ),
     )(
         prompt, norm_gain[None, :], w_query, w_key, w_value, query_gain[None, :], key_gain[None, :], table,
-        sampled.reshape(64, 1), near_c, near_s, far_c, far_s, spread.astype(jnp.bfloat16),
+        sampled.T, near_c, near_s, far_c, far_s, spread.astype(jnp.bfloat16),
     )
     return out, dec[None, :4]
 

time: 111 us -> 80 us (0.72)
  the two profiles are of different devices: /device:TPU:1 before, /device:TPU:110 now
where the time goes in v2:
time: 80 us; the launch traced here: 79.7 us
  Pallas kernels  75.5 us (94%)
  local copies, waits for them, and re-layouts  3.58 us (4%)
    pallas_call x1, Pallas kernels, body(): pl.pallas_call(kernel, out_shape=(jax.ShapeDtypeStruct((ROWS, HEADS * HD)...  75.5 us
    unnamed x1, local copies, waits for them, and re-layouts  2.26 us

profile of v2, /device:TPU:110, one launch (start us, length us, event | category | flops | bytes accessed | tf_op | source)
XLA Modules:
  0.0 79.7 jit_solution(13765613762970031055)
XLA Ops:
  0.6 75.5 %shard_map.149 = (bf16[512,1024]{1,0:T(8,128)(2,1)}, bf16[16,1024]{1,0:T(8,128)(2,1)}) custom-call(bf16[512,5120]{1,0:T(8,128)(2,1)} %prompt.1, f32[1,5120]{1,0:T(1,128)} %bitcast.6, bf16[5120,1024]{1,0:T(8,128)(2,1)} %w_query.1, bf16[5120,128]{1,0:T(8,128)(2,1)} %w_key.1, bf16[5120,128]{1,0:T(8,128)(2,1)} %w_value.1, f32[1,128]{1,0:T(1,128)} %bitcast.8, ...), custom_call_target="tpu_custom_call" | custom-call | tf_op jit(solution)/shard_map/pallas_call | solution.py:526
  76.2 1.3 %slice_bitcast_fusion = bf16[1,4,1024]{2,1,0:T(4,128)(2,1)} fusion(bf16[16,1024]{1,0:T(8,128)(2,1)} %get-tuple-element.5), kind=kLoop, calls=%fused_computation | loop fusion | bytes 16384 | tf_op jit(solution)/shard_map/broadcast_in_dim | solution.py:567
  77.5 2.3 %copy.17 = bf16[512,1024]{1,0:T(8,128)(2,1)} copy(bf16[512,1024]{1,0:T(8,128)(2,1)} %get-tuple-element.8) | data formatting | bytes 2097152

commit v3 on v2

--- a/solution.py
+++ b/solution.py
@@ -24,7 +24,7 @@
 LOW = -1e30
 GROUP = 5
 SPARE = 11
-TAKEN = (3, 3, 2, 1)
+TAKEN = (3, 3, 2, 1, 2, 1, 3, 3)
 ACC = HD + 16
 
 
@@ -45,8 +45,8 @@
     soon = [at(0, 1 - yy), at(3, yy), at(1, yy), at(2, yy)]
     late = [at(3, 1 - yy), at(1, 1 - yy), at(2, 1 - yy)]
     cut = lambda pairs, limit: [j for j in pairs if j < limit]
-    lists = [cut(soon, chip), cut(late, chip)]
-    lists += [cut([chip] + soon, 7 - chip), cut(late, 7 - chip)] if chip < 4 else [[], []]
+    other = (3 - zz) * 2 + yy if chip < 4 else -1
+    lists = [cut(soon, chip), cut([chip] + soon, other), cut(late, other), cut(late, chip)]
     return [(len(pairs), sum(j << (3 * k) for k, j in enumerate(pairs))) for pairs in lists]
 
 
@@ -63,8 +63,8 @@
 def kernel(
     prompt, gain, w_query, w_key, w_value, q_gain, k_gain, table, ids, near_c, near_s, far_c, far_s, spread,
     out, dec,
-    x, wq, wkv, tab, q, kbuf, vbuf, acc, top, es, er, eb, ec, eh, xs, qd, accd, topd, fsend, frecv,
-    load_sem, wq_sem, ks, kr, vs, vr, e1s, e1r, e2s, e2r, e3s, e3r, qs, qr, fs, fr,
+    x, wq, wkv, tab, q, kbuf, vbuf, acc, top, es, e0, er, eb, ec, eh, xs, qd, accd, topd, fsend, frecv,
+    load_sem, wq_sem, ks, kr, vs, vr, e0r, e1s, e1r, e2s, e2r, e3s, e3r, qs, qr, fs, fr,
 ):
     ctx = lax.axis_index("ctx")
     tp = lax.axis_index("tp")
@@ -201,8 +201,8 @@
     hop_own()
 
     light = chip < 4
-    moved = pick(chip, TAKEN + TAKEN[::-1])
-    partner = block(3 - z, 1 - yh, core)
+    moved = pick(chip, TAKEN)
+    partner = block(3 - z, yh, core)
     kept = jnp.where(light, HEADS, HEADS - moved)
 
     def project_queries(first):
@@ -215,6 +215,11 @@
 
     def query_copy(f):
         return remote(q.at[kept + f], q.at[HEADS + f], qs.at[f], qr.at[f], partner, tp)
+
+    hop_ring()
+    query_loads[1].wait()
+    project_queries(0)
+    hop_across()
 
     @pl.when(jnp.logical_not(light))
     def _():
@@ -222,110 +227,133 @@
         def _(f):
             query_copy(f).start()
 
-    query_loads[1].wait()
-    project_queries(0)
     table_load.wait()
     first_row = (ctx * NTP + tp) * VROWS
     lanes = (lax.broadcasted_iota(jnp.int32, (16, VROWS), 1) + first_row).astype(jnp.float32)
-    diagonal = lax.broadcasted_iota(jnp.int32, (16, 16), 0) == lax.broadcasted_iota(jnp.int32, (16, 16), 1)
+    down = lax.broadcasted_iota(jnp.int32, (16, 16), 0)
+    sample = down % 8 * 2 + down // 8
+    chosen = sample == lax.broadcasted_iota(jnp.int32, (16, 16), 1)
     picks = []
     for j in range(4):
-        wanted = jnp.where(diagonal, ids[j:j + 1, :].astype(jnp.float32), 0.0)
+        wanted = jnp.where(chosen, ids[j:j + 1, :].astype(jnp.float32), 0.0)
         picks.append((jnp.sum(wanted, axis=1, keepdims=True) == lanes).astype(jnp.float32))
-    picks = jnp.concatenate(picks, axis=0).astype(jnp.bfloat16)
-    for n in range(NTP):
-        cols = slice(n * PIECE, (n + 1) * PIECE)
-        es[n] = jnp.dot(picks, tab[:, cols], preferred_element_type=jnp.float32).astype(jnp.bfloat16)
-    er[tp] = es[tp]
-
-    @pl.loop(1, NTP)
-    def _(i):
-        to = (tp + i) % NTP
-        remote(es.at[to], er.at[tp], e1s.at[i], e1r.at[tp], ctx, to).start()
-
-    ones = jnp.ones((16, PAIR), jnp.bfloat16)
+    for c in range(2):
+        rows = jnp.concatenate([p[c * 8:(c + 1) * 8] for p in picks], axis=0).astype(jnp.bfloat16)
+        for n in range(NTP):
+            cols = slice(n * PIECE, (n + 1) * PIECE)
+            es[c, n] = jnp.dot(rows, tab[:, cols], preferred_element_type=jnp.float32).astype(jnp.bfloat16)
+
+    def core_copy():
+        return remote(es.at[1 - core], e0, e1s.at[0], e0r, sib, tp)
+
+    core_copy().start()
 
     def pair_keys(j):
         return kbuf[pl.ds(2 * j, 2)].reshape(PAIR, HD)
 
+    def with_ones(values):
+        return jnp.concatenate([values, jnp.ones((16, values.shape[1]), jnp.bfloat16)], axis=0)
+
     def pair_values(j):
-        values = jnp.concatenate([vbuf[2 * j], vbuf[2 * j + 1]], axis=1)
-        return jnp.concatenate([values, ones], axis=0)
+        return with_ones(jnp.concatenate([vbuf[2 * j], vbuf[2 * j + 1]], axis=1))
 
     def scores(keys, queries):
         return lax.dot_general(keys, queries, (((1,), (1,)), ((), ())), preferred_element_type=jnp.float32)
 
-    def pipeline(units, first, second, third):
+    def pipeline(units):
         held, mixed = {}, {}
         count = len(units)
         for t in range(count + 2):
             if t < count:
-                held[t] = first(units[t])
+                held[t] = units[t][0]()
             if 0 <= t - 2:
-                third(units[t - 2], mixed.pop(t - 2))
+                units[t - 2][2](mixed.pop(t - 2))
             if 0 <= t - 1 < count:
-                mixed[t - 1] = second(units[t - 1], held.pop(t - 1))
-
-    def unit_scores(unit):
-        j, source, _ = unit
-        return scores(pair_keys(j), q[source])
+                mixed[t - 1] = units[t - 1][1](held.pop(t - 1))
+
+    def causal(s):
+        down = lax.broadcasted_iota(jnp.int32, s.shape, 0)
+        return jnp.where(down <= lax.broadcasted_iota(jnp.int32, s.shape, 1), s, LOW)
+
+    def open_unit(source, slot):
+        def first():
+            return scores(kbuf[ctx], q[source])
+
+        def second(s):
+            s = causal(s)
+            peak = jnp.max(s, axis=0, keepdims=True) * SCALE
+            top[slot, :1, :] = peak
+            return jnp.exp2(s * SCALE - peak).astype(jnp.bfloat16)
+
+        def third(w):
+            acc[slot] = jnp.dot(with_ones(vbuf[ctx]), w, preferred_element_type=jnp.float32)
+
+        return first, second, third
+
+    def next_unit(keys, values, source, slot, mask=None):
+        def first():
+            return scores(keys(), q[source])
+
+        def second(s):
+            if mask is not None:
+                s = mask(s)
+            before = top[slot, :1, :]
+            peak = jnp.maximum(before, jnp.max(s, axis=0, keepdims=True) * SCALE)
+            top[slot, :1, :] = peak
+            return jnp.exp2(s * SCALE - peak).astype(jnp.bfloat16), jnp.exp2(before - peak)
+
+        def third(weights):
+            w, factor = weights
+            acc[slot] = acc[slot] * factor + jnp.dot(values(), w, preferred_element_type=jnp.float32)
+
+        return first, second, third
+
+    def pair_unit(j, source, slot):
+        return next_unit(lambda: pair_keys(j), lambda: pair_values(j), source, slot)
+
+    def block_unit(b, source, slot, mask=None):
+        return next_unit(lambda: kbuf[b], lambda: with_ones(vbuf[b]), source, slot, mask)
+
+    def open_heads(begin, width, count):
+        places = []
+        for n in range(width):
+            use = n < count
+            places.append((jnp.where(use, begin + n, 0), jnp.where(use, begin + n, SPARE)))
+
+        @pl.when(core == 0)
+        def _():
+            pipeline([open_unit(*place) for place in places])
+
+        @pl.when(core == 1)
+        def _():
+            pipeline([open_unit(*place) for place in places] + [block_unit(sib, *place) for place in places])
 
     arrived("k", sib)
     arrived("v", sib)
-    later = lax.broadcasted_iota(jnp.int32, (PAIR, ROWS), 0) - lax.broadcasted_iota(jnp.int32, (PAIR, ROWS), 1)
-
-    def open_weights(unit, s):
-        s = jnp.where(later <= core * ROWS, s, LOW)
-        peak = jnp.max(s, axis=0, keepdims=True) * SCALE
-        top[unit[2], :1, :] = peak
-        return jnp.exp2(s * SCALE - peak).astype(jnp.bfloat16)
-
-    def open_mix(unit, weights):
-        acc[unit[2]] = jnp.dot(pair_values(unit[0]), weights, preferred_element_type=jnp.float32)
-
-    def next_weights(unit, s):
-        before = top[unit[2], :1, :]
-        peak = jnp.maximum(before, jnp.max(s, axis=0, keepdims=True) * SCALE)
-        top[unit[2], :1, :] = peak
-        return jnp.exp2(s * SCALE - peak).astype(jnp.bfloat16), jnp.exp2(before - peak)
-
-    def last_weights(unit, s):
-        return next_weights(unit, jnp.where(later <= core * ROWS, s, LOW))
-
-    def next_mix(unit, weights):
-        w, factor = weights
-        slot = unit[2]
-        acc[slot] = acc[slot] * factor + jnp.dot(pair_values(unit[0]), w, preferred_element_type=jnp.float32)
-
-    def open_heads(begin, count):
-        units = []
-        for n in range(4):
-            use = n < count
-            units.append((chip, jnp.where(use, begin + n, 0), jnp.where(use, begin + n, SPARE)))
-        pipeline(units, unit_scores, open_weights, open_mix)
-
-    open_heads(chip * 0, chip * 0 + 4)
-    hop_ring()
-    open_heads(chip * 0 + 4, kept - 4)
-    hop_across()
+    hop_last(block(z2, yh, core), across)
+    open_heads(chip * 0, 4, kept)
+    core_copy().wait_recv()
+    for n in range(NTP):
+        e0[n] = (e0[n].astype(jnp.float32) + es[core, n].astype(jnp.float32)).astype(jnp.bfloat16)
+    er[tp] = e0[tp]
+
+    def token_copy(i, to, frm):
+        return remote(e0.at[to], er.at[frm], e1s.at[i], e1r.at[frm], ctx, to)
+
     @pl.loop(1, NTP)
     def _(i):
-        frm = (tp + i) % NTP
-        remote(es.at[frm], er.at[frm], e1s.at[i], e1r.at[frm], ctx, frm).wait_recv()
-
-    piece = er[0].astype(jnp.float32)
-    for n in range(1, NTP):
-        piece = piece + er[n].astype(jnp.float32)
-    piece = jnp.dot(spread[...], piece.astype(jnp.bfloat16), preferred_element_type=jnp.float32)
-    eb[...] = piece.astype(jnp.bfloat16).reshape(NCTX, 16, PIECE)
-    ec[ctx] = eb[ctx]
-
-    @pl.loop(1, NCTX)
-    def _(i):
-        to = (ctx + i) % NCTX
-        remote(eb.at[to], ec.at[ctx], e2s.at[i], e2r.at[ctx], to, tp).start()
-
-    hop_last(block(z2, yh, core), across)
+        token_copy(i, (tp + i) % NTP, tp).start()
+
+    @pl.when(kept > 6)
+    def _():
+        open_heads(chip * 0 + 4, 4, kept - 4)
+
+    @pl.when(kept <= 6)
+    def _():
+        open_heads(chip * 0 + 4, 2, kept - 4)
+
+    hop_last(late_left)
+    hop_last(late_right)
     for zz, yy in ((z, 1 - yh), (zm, yh), (zp, yh), (z2, yh)):
         from_sib(zz, yy)
 
@@ -333,82 +361,107 @@
     def _():
         @pl.loop(0, moved)
         def _(f):
-            query_copy(f).wait_recv()
             acc[HEADS + f] = jnp.zeros((ACC, ROWS), jnp.float32)
             top[HEADS + f] = jnp.full((8, ROWS), LOW, jnp.float32)
 
     acc[SPARE] = jnp.zeros((ACC, ROWS), jnp.float32)
     top[SPARE] = jnp.zeros((8, ROWS), jnp.float32)
 
-    def settle(turn, k, h, sizes):
-        for n in range(2):
-            end = (turn == n) & (k >= sizes[n])
+    counts = [pick(chip, [lists[n][0] for lists in PAIR_LISTS]) for n in range(4)]
+    codes = [pick(chip, [lists[n][1] for lists in PAIR_LISTS]) for n in range(4)]
+    widths = [kept, moved, moved, kept]
+    soon_units = counts[0] * kept + counts[1] * moved
+    all_units = soon_units + counts[2] * moved + counts[3] * kept
+    late_group = soon_units // GROUP
+
+    def choose(turn, values):
+        result = values[0]
+        for n in range(1, 4):
+            result = jnp.where(turn == n, values[n], result)
+        return result
+
+    def settle(turn, k, h):
+        for n in range(4):
+            end = (turn == n) & (k >= counts[n])
             turn = jnp.where(end, n + 1, turn)
             k = jnp.where(end, 0, k)
         return turn, k, h
 
-    def run_pairs(own_list, other_list, own_first, between=None):
-        tables = [[PAIR_LISTS[c][n] for c in range(8)] for n in (own_list, other_list)]
-        sizes = [pick(chip, [entry[0] for entry in t]) for t in tables]
-        codes = [pick(chip, [entry[1] for entry in t]) for t in tables]
-        widths, bases = [kept, moved], [chip * 0, chip * 0 + HEADS]
-        if not own_first:
-            for items in (sizes, codes, widths, bases):
-                items.reverse()
-        total = sizes[0] * widths[0] + sizes[1] * widths[1]
-
-        def step(g, state):
-            if between is not None:
-                between(g)
-            units = []
-            for n in range(GROUP):
-                turn, k, h = state
-                first = turn == 0
-                use = turn < 2
-                j = lax.shift_right_logical(jnp.where(first, codes[0], codes[1]), 3 * k) % 8
-                slot = jnp.where(first, bases[0], bases[1]) + h
-                units.append((jnp.where(use, j, chip), jnp.where(use, slot, 0), jnp.where(use, slot, SPARE)))
-                h = h + 1
-                wrap = h >= jnp.where(first, widths[0], widths[1])
-                state = settle(turn, k + wrap.astype(jnp.int32), jnp.where(wrap, 0, h), sizes)
-            pipeline(units, unit_scores, next_weights, next_mix)
-            return state
-
-        start = settle(chip * 0, chip * 0, chip * 0, sizes)
-        lax.fori_loop(0, (total + GROUP - 1) // GROUP, step, start)
-
-    def hops_between(g):
-        @pl.when(g == 1)
-        def _():
-            hop_last(late_left)
-            hop_last(late_right)
-
-        @pl.when(g == 2)
-        def _():
-            hop_last(late_far)
-
-    run_pairs(0, 2, True, hops_between)
-
-    @pl.loop(1, NCTX)
-    def _(i):
-        frm = (ctx + i) % NCTX
-        remote(eb.at[frm], ec.at[frm], e2s.at[i], e2r.at[frm], frm, tp).wait_recv()
-
-    piece = ec[0].astype(jnp.float32)
-    for n in range(1, NCTX):
-        piece = piece + ec[n].astype(jnp.float32)
-    eh[tp] = piece.astype(jnp.bfloat16)
+    def sample_copy(i, to, frm):
+        return remote(eb.at[to], ec.at[frm], e2s.at[i], e2r.at[frm], to * 2 + core, tp)
+
+    def sum_tokens():
+        @pl.loop(1, NTP)
+        def _(i):
+            frm = (tp + i) % NTP
+            token_copy(i, frm, frm).wait_recv()
+
+        piece = er[0].astype(jnp.float32)
+        for n in range(1, NTP):
+            piece = piece + er[n].astype(jnp.float32)
+        piece = jnp.dot(spread[...], piece.astype(jnp.bfloat16), preferred_element_type=jnp.float32)
+        eb[...] = piece.astype(jnp.bfloat16).reshape(8, 16, PIECE)
+        ec[chip] = eb[chip]
+
+        @pl.loop(1, 8)
+        def _(i):
+            sample_copy(i, (chip + i) % 8, chip).start()
 
     def piece_copy(i, to, frm):
         return remote(eh.at[frm], eh.at[frm], e3s.at[i], e3r.at[frm], ctx, to)
 
-    @pl.loop(1, NTP)
-    def _(i):
-        piece_copy(i, (tp + i) % NTP, tp).start()
-
-    for zz in (zm, zp, z2):
-        from_sib(zz, 1 - yh)
-    run_pairs(1, 3, False)
+    def sum_samples():
+        @pl.loop(1, 8)
+        def _(i):
+            frm = (chip + i) % 8
+            sample_copy(i, frm, frm).wait_recv()
+
+        piece = ec[0].astype(jnp.float32)
+        for n in range(1, 8):
+            piece = piece + ec[n].astype(jnp.float32)
+        eh[tp] = piece.astype(jnp.bfloat16)
+
+        @pl.loop(1, NTP)
+        def _(i):
+            piece_copy(i, (tp + i) % NTP, tp).start()
+
+    def between(g):
+        @pl.when(light & (g == jnp.minimum(chip, 1)))
+        def _():
+            @pl.loop(0, moved)
+            def _(f):
+                query_copy(f).wait_recv()
+
+        @pl.when(g == 1)
+        def _():
+            hop_last(late_far)
+            sum_tokens()
+
+        @pl.when(g == late_group)
+        def _():
+            for zz in (zm, zp, z2):
+                from_sib(zz, 1 - yh)
+
+        @pl.when(g == late_group + 1)
+        def _():
+            sum_samples()
+
+    def step(g, state):
+        between(g)
+        units = []
+        for n in range(GROUP):
+            turn, k, h = state
+            use = turn < 4
+            j = lax.shift_right_logical(choose(turn, codes), 3 * k) % 8
+            slot = h + jnp.where((turn == 1) | (turn == 2), HEADS, 0 * h)
+            units.append(pair_unit(jnp.where(use, j, chip), jnp.where(use, slot, 0), jnp.where(use, slot, SPARE)))
+            h = h + 1
+            wrap = h >= choose(turn, widths)
+            state = settle(turn, k + wrap.astype(jnp.int32), jnp.where(wrap, 0, h))
+        pipeline(units)
+        return state
+
+    lax.fori_loop(0, (all_units + GROUP - 1) // GROUP, step, settle(chip * 0, chip * 0, chip * 0))
 
     def finished(slot):
         mix = acc[slot]
@@ -419,12 +472,31 @@
 
     @pl.when(light)
     def _():
-        units = []
-        for f in range(3):
-            use = f < moved
-            slot = HEADS + f + 0 * chip
-            units.append((7 - chip, jnp.where(use, slot, 0), jnp.where(use, slot, SPARE)))
-        pipeline(units, unit_scores, last_weights, next_mix)
+        def close_heads(width):
+            places = []
+            for f in range(width):
+                use = f < moved
+                slot = HEADS + f + 0 * chip
+                places.append((jnp.where(use, slot, 0), jnp.where(use, slot, SPARE)))
+
+            @pl.when(core == 0)
+            def _():
+                pipeline([block_unit(partner, *place, causal) for place in places])
+
+            @pl.when(core == 1)
+            def _():
+                pipeline(
+                    [block_unit(partner, *place, causal) for place in places]
+                    + [block_unit(partner - 1, *place) for place in places]
+                )
+
+        @pl.when(moved == 1)
+        def _():
+            close_heads(1)
+
+        @pl.when(moved > 1)
+        def _():
+            close_heads(3)
 
         @pl.loop(0, moved)
         def _(f):
@@ -461,20 +533,23 @@
         step_values, weights, (((0,), (0,)), ((), ())), preferred_element_type=jnp.float32
     )
 
-    def step_weights(j, s):
-        before = topd[:1, :]
-        peak = jnp.maximum(before, jnp.max(s, axis=0, keepdims=True) * SCALE)
-        topd[:1, :] = peak
-        return jnp.exp2(s * SCALE - peak).astype(jnp.bfloat16), jnp.exp2(before - peak)
-
-    def step_mix(j, weights):
-        w, factor = weights
-        accd[...] = accd[...] * factor + jnp.dot(pair_values(j), w, preferred_element_type=jnp.float32)
-
-    @pl.loop(0, 2)
-    def _(g):
-        pipeline([g * 4 + n for n in range(4)], lambda j: scores(pair_keys(j), qd[...]), step_weights, step_mix)
-
+    def step_unit(j):
+        def first():
+            return scores(pair_keys(j), qd[...])
+
+        def second(s):
+            before = topd[:1, :]
+            peak = jnp.maximum(before, jnp.max(s, axis=0, keepdims=True) * SCALE)
+            topd[:1, :] = peak
+            return jnp.exp2(s * SCALE - peak).astype(jnp.bfloat16), jnp.exp2(before - peak)
+
+        def third(weights):
+            w, factor = weights
+            accd[...] = accd[...] * factor + jnp.dot(pair_values(j), w, preferred_element_type=jnp.float32)
+
+        return first, second, third
+
+    pipeline([step_unit(j) for j in range(8)])
     mix = accd[...]
     steps = (mix[:HD] * (1.0 / mix[HD:HD + 1])).T.astype(jnp.bfloat16)
     for h in range(HEADS):
@@ -501,24 +576,25 @@
     for item in sent:
         block_copy(*item).wait_send()
 
+    core_copy().wait_send()
+
     @pl.loop(1, NTP)
     def _(i):
         to = (tp + i) % NTP
-        remote(es.at[to], er.at[tp], e1s.at[i], e1r.at[tp], ctx, to).wait_send()
+        token_copy(i, to, tp).wait_send()
         piece_copy(i, to, tp).wait_send()
 
-    @pl.loop(1, NCTX)
+    @pl.loop(1, 8)
     def _(i):
-        to = (ctx + i) % NCTX
-        remote(eb.at[to], ec.at[ctx], e2s.at[i], e2r.at[ctx], to, tp).wait_send()
+        sample_copy(i, (chip + i) % 8, chip).wait_send()
 
 
 def body(prompt, norm_gain, w_query, w_key, w_value, query_gain, key_gain, table, sampled):
     near_c, near_s, far_c, far_s = rope_tables(NCTX * ROWS)
-    spread = np.zeros((NCTX * 16, 64), np.float32)
-    for s in range(NCTX):
+    spread = np.zeros((8 * 16, 32), np.float32)
+    for s in range(8):
         for j in range(4):
-            spread[s * 16 + j, j * 16 + s] = 1.0
+            spread[s * 16 + j, j * 8 + s] = 1.0
     hbm = pl.BlockSpec(memory_space=pl.ANY)
     vmem = pl.BlockSpec(memory_space=pltpu.VMEM)
     bf, f32 = jnp.bfloat16, jnp.float32
@@ -541,10 +617,11 @@
             pltpu.VMEM((NCTX, HD, ROWS), bf),
             pltpu.VMEM((SPARE + 1, ACC, ROWS), f32),
             pltpu.VMEM((SPARE + 1, 8, ROWS), f32),
-            pltpu.VMEM((NTP, 64, PIECE), bf),
-            pltpu.VMEM((NTP, 64, PIECE), bf),
-            pltpu.VMEM((NCTX, 16, PIECE), bf),
-            pltpu.VMEM((NCTX, 16, PIECE), bf),
+            pltpu.VMEM((2, NTP, 32, PIECE), bf),
+            pltpu.VMEM((NTP, 32, PIECE), bf),
+            pltpu.VMEM((NTP, 32, PIECE), bf),
+            pltpu.VMEM((8, 16, PIECE), bf),
+            pltpu.VMEM((8, 16, PIECE), bf),
             pltpu.VMEM((NTP, 16, PIECE), bf),
             pltpu.VMEM((16, D), bf),
             pltpu.VMEM((HD, HD), bf),
@@ -554,7 +631,7 @@
             pltpu.VMEM((4, ROWS, HD), bf),
             dma((7,)), dma((2,)),
             dma((16,)), dma((NCTX,)), dma((16,)), dma((NCTX,)),
-            dma((NTP,)), dma((NTP,)), dma((NCTX,)), dma((NCTX,)), dma((NTP,)), dma((NTP,)),
+            dma, dma((NTP,)), dma((NTP,)), dma((8,)), dma((8,)), dma((NTP,)), dma((NTP,)),
             dma((4,)), dma((4,)), dma((4,)), dma((4,)),
         ],
         compiler_params=pltpu.CompilerParams(

time: 80 us -> 72.8 us (0.910)
  the two profiles are of different devices: /device:TPU:110 before, /device:TPU:18 now
where the time goes in v3:
time: 72.8 us; the launch traced here: 72.1 us
  Pallas kernels  67.9 us (93%)
  local copies, waits for them, and re-layouts  3.58 us (5%)
    pallas_call x1, Pallas kernels, body(): pl.pallas_call(kernel, out_shape=(jax.ShapeDtypeStruct((ROWS, HEADS * HD)...  67.9 us
    unnamed x1, local copies, waits for them, and re-layouts  2.26 us

profile of v3, /device:TPU:18, one launch (start us, length us, event | category | flops | bytes accessed | tf_op | source)
XLA Modules:
  0.0 72.1 jit_solution(9454326157208266781)
XLA Ops:
  0.6 67.9 %shard_map.149 = (bf16[512,1024]{1,0:T(8,128)(2,1)}, bf16[16,1024]{1,0:T(8,128)(2,1)}) custom-call(bf16[512,5120]{1,0:T(8,128)(2,1)} %prompt.1, f32[1,5120]{1,0:T(1,128)} %bitcast.6, bf16[5120,1024]{1,0:T(8,128)(2,1)} %w_query.1, bf16[5120,128]{1,0:T(8,128)(2,1)} %w_key.1, bf16[5120,128]{1,0:T(8,128)(2,1)} %w_value.1, f32[1,128]{1,0:T(1,128)} %bitcast.8, ...), custom_call_target="tpu_custom_call" | custom-call | tf_op jit(solution)/shard_map/pallas_call | solution.py:602
  68.5 1.3 %slice_bitcast_fusion = bf16[1,4,1024]{2,1,0:T(4,128)(2,1)} fusion(bf16[16,1024]{1,0:T(8,128)(2,1)} %get-tuple-element.5), kind=kLoop, calls=%fused_computation | loop fusion | bytes 16384 | tf_op jit(solution)/shard_map/broadcast_in_dim | solution.py:644
  69.9 2.3 %copy.17 = bf16[512,1024]{1,0:T(8,128)(2,1)} copy(bf16[512,1024]{1,0:T(8,128)(2,1)} %get-tuple-element.8) | data formatting | bytes 2097152

commit v4 on v3

--- a/solution.py
+++ b/solution.py
@@ -227,6 +227,92 @@
         def _(f):
             query_copy(f).start()
 
+
+    def pair_keys(j):
+        return kbuf[pl.ds(2 * j, 2)].reshape(PAIR, HD)
+
+    def with_ones(values):
+        return jnp.concatenate([values, jnp.ones((16, values.shape[1]), jnp.bfloat16)], axis=0)
+
+    def pair_values(j):
+        return with_ones(jnp.concatenate([vbuf[2 * j], vbuf[2 * j + 1]], axis=1))
+
+    def scores(keys, queries):
+        return lax.dot_general(keys, queries, (((1,), (1,)), ((), ())), preferred_element_type=jnp.float32)
+
+    def pipeline(units):
+        held, mixed = {}, {}
+        count = len(units)
+        for t in range(count + 2):
+            if t < count:
+                held[t] = units[t][0]()
+            if 0 <= t - 2:
+                units[t - 2][2](mixed.pop(t - 2))
+            if 0 <= t - 1 < count:
+                mixed[t - 1] = units[t - 1][1](held.pop(t - 1))
+
+    def causal(s):
+        down = lax.broadcasted_iota(jnp.int32, s.shape, 0)
+        return jnp.where(down <= lax.broadcasted_iota(jnp.int32, s.shape, 1), s, LOW)
+
+    def open_unit(source, slot):
+        def first():
+            return scores(kbuf[ctx], q[source])
+
+        def second(s):
+            s = causal(s)
+            peak = jnp.max(s, axis=0, keepdims=True) * SCALE
+            top[slot, :1, :] = peak
+            return jnp.exp2(s * SCALE - peak).astype(jnp.bfloat16)
+
+        def third(w):
+            acc[slot] = jnp.dot(with_ones(vbuf[ctx]), w, preferred_element_type=jnp.float32)
+
+        return first, second, third
+
+    def next_unit(keys, values, source, slot, mask=None):
+        def first():
+            return scores(keys(), q[source])
+
+        def second(s):
+            if mask is not None:
+                s = mask(s)
+            before = top[slot, :1, :]
+            peak = jnp.maximum(before, jnp.max(s, axis=0, keepdims=True) * SCALE)
+            top[slot, :1, :] = peak
+            return jnp.exp2(s * SCALE - peak).astype(jnp.bfloat16), jnp.exp2(before - peak)
+
+        def third(weights):
+            w, factor = weights
+            acc[slot] = acc[slot] * factor + jnp.dot(values(), w, preferred_element_type=jnp.float32)
+
+        return first, second, third
+
+    def pair_unit(j, source, slot):
+        return next_unit(lambda: pair_keys(j), lambda: pair_values(j), source, slot)
+
+    def block_unit(b, source, slot, mask=None):
+        return next_unit(lambda: kbuf[b], lambda: with_ones(vbuf[b]), source, slot, mask)
+
+    def open_heads(begin, width, count):
+        places = []
+        for n in range(width):
+            use = n < count
+            places.append((jnp.where(use, begin + n, 0), jnp.where(use, begin + n, SPARE)))
+
+        @pl.when(core == 0)
+        def _():
+            pipeline([open_unit(*place) for place in places])
+
+        @pl.when(core == 1)
+        def _():
+            pipeline([open_unit(*place) for place in places] + [block_unit(sib, *place) for place in places])
+
+    arrived("k", sib)
+    arrived("v", sib)
+    hop_last(block(z2, yh, core), across)
+    open_heads(chip * 0, 4, kept)
+
     table_load.wait()
     first_row = (ctx * NTP + tp) * VROWS
     lanes = (lax.broadcasted_iota(jnp.int32, (16, VROWS), 1) + first_row).astype(jnp.float32)
@@ -248,90 +334,14 @@
 
     core_copy().start()
 
-    def pair_keys(j):
-        return kbuf[pl.ds(2 * j, 2)].reshape(PAIR, HD)
-
-    def with_ones(values):
-        return jnp.concatenate([values, jnp.ones((16, values.shape[1]), jnp.bfloat16)], axis=0)
-
-    def pair_values(j):
-        return with_ones(jnp.concatenate([vbuf[2 * j], vbuf[2 * j + 1]], axis=1))
-
-    def scores(keys, queries):
-        return lax.dot_general(keys, queries, (((1,), (1,)), ((), ())), preferred_element_type=jnp.float32)
-
-    def pipeline(units):
-        held, mixed = {}, {}
-        count = len(units)
-        for t in range(count + 2):
-            if t < count:
-                held[t] = units[t][0]()
-            if 0 <= t - 2:
-                units[t - 2][2](mixed.pop(t - 2))
-            if 0 <= t - 1 < count:
-                mixed[t - 1] = units[t - 1][1](held.pop(t - 1))
-
-    def causal(s):
-        down = lax.broadcasted_iota(jnp.int32, s.shape, 0)
-        return jnp.where(down <= lax.broadcasted_iota(jnp.int32, s.shape, 1), s, LOW)
-
-    def open_unit(source, slot):
-        def first():
-            return scores(kbuf[ctx], q[source])
-
-        def second(s):
-            s = causal(s)
-            peak = jnp.max(s, axis=0, keepdims=True) * SCALE
-            top[slot, :1, :] = peak
-            return jnp.exp2(s * SCALE - peak).astype(jnp.bfloat16)
-
-        def third(w):
-            acc[slot] = jnp.dot(with_ones(vbuf[ctx]), w, preferred_element_type=jnp.float32)
-
-        return first, second, third
-
-    def next_unit(keys, values, source, slot, mask=None):
-        def first():
-            return scores(keys(), q[source])
-
-        def second(s):
-            if mask is not None:
-                s = mask(s)
-            before = top[slot, :1, :]
-            peak = jnp.maximum(before, jnp.max(s, axis=0, keepdims=True) * SCALE)
-            top[slot, :1, :] = peak
-            return jnp.exp2(s * SCALE - peak).astype(jnp.bfloat16), jnp.exp2(before - peak)
-
-        def third(weights):
-            w, factor = weights
-            acc[slot] = acc[slot] * factor + jnp.dot(values(), w, preferred_element_type=jnp.float32)
-
-        return first, second, third
-
-    def pair_unit(j, source, slot):
-        return next_unit(lambda: pair_keys(j), lambda: pair_values(j), source, slot)
-
-    def block_unit(b, source, slot, mask=None):
-        return next_unit(lambda: kbuf[b], lambda: with_ones(vbuf[b]), source, slot, mask)
-
-    def open_heads(begin, width, count):
-        places = []
-        for n in range(width):
-            use = n < count
-            places.append((jnp.where(use, begin + n, 0), jnp.where(use, begin + n, SPARE)))
-
-        @pl.when(core == 0)
-        def _():
-            pipeline([open_unit(*place) for place in places])
-
-        @pl.when(core == 1)
-        def _():
-            pipeline([open_unit(*place) for place in places] + [block_unit(sib, *place) for place in places])
-
-    arrived("k", sib)
-    arrived("v", sib)
-    hop_last(block(z2, yh, core), across)
-    open_heads(chip * 0, 4, kept)
+    @pl.when(kept > 6)
+    def _():
+        open_heads(chip * 0 + 4, 4, kept - 4)
+
+    @pl.when(kept <= 6)
+    def _():
+        open_heads(chip * 0 + 4, 2, kept - 4)
+
     core_copy().wait_recv()
     for n in range(NTP):
         e0[n] = (e0[n].astype(jnp.float32) + es[core, n].astype(jnp.float32)).astype(jnp.bfloat16)
@@ -344,16 +354,6 @@
     def _(i):
         token_copy(i, (tp + i) % NTP, tp).start()
 
-    @pl.when(kept > 6)
-    def _():
-        open_heads(chip * 0 + 4, 4, kept - 4)
-
-    @pl.when(kept <= 6)
-    def _():
-        open_heads(chip * 0 + 4, 2, kept - 4)
-
-    hop_last(late_left)
-    hop_last(late_right)
     for zz, yy in ((z, 1 - yh), (zm, yh), (zp, yh), (z2, yh)):
         from_sib(zz, yy)
 
@@ -434,7 +434,12 @@
 
         @pl.when(g == 1)
         def _():
+            hop_last(late_left)
+            hop_last(late_right)
             hop_last(late_far)
+
+        @pl.when(g == 2)
+        def _():
             sum_tokens()
 
         @pl.when(g == late_group)

time: 72.8 us -> 71.8 us (0.986)
  no operation moved by 1% of the time
where the time goes in v4:
time: 71.8 us; the launch traced here: 71.6 us
  Pallas kernels  67.4 us (94%)
  local copies, waits for them, and re-layouts  3.58 us (5%)
    pallas_call x1, Pallas kernels, body(): pl.pallas_call(kernel, out_shape=(jax.ShapeDtypeStruct((ROWS, HEADS * HD)...  67.4 us
    unnamed x1, local copies, waits for them, and re-layouts  2.26 us

profile of v4, /device:TPU:18, one launch (start us, length us, event | category | flops | bytes accessed | tf_op | source)
XLA Modules:
  0.0 71.6 jit_solution(3670794481441008074)
XLA Ops:
  0.6 67.4 %shard_map.149 = (bf16[512,1024]{1,0:T(8,128)(2,1)}, bf16[16,1024]{1,0:T(8,128)(2,1)}) custom-call(bf16[512,5120]{1,0:T(8,128)(2,1)} %prompt.1, f32[1,5120]{1,0:T(1,128)} %bitcast.6, bf16[5120,1024]{1,0:T(8,128)(2,1)} %w_query.1, bf16[5120,128]{1,0:T(8,128)(2,1)} %w_key.1, bf16[5120,128]{1,0:T(8,128)(2,1)} %w_value.1, f32[1,128]{1,0:T(1,128)} %bitcast.8, ...), custom_call_target="tpu_custom_call" | custom-call | tf_op jit(solution)/shard_map/pallas_call | solution.py:607
  68.0 1.3 %slice_bitcast_fusion = bf16[1,4,1024]{2,1,0:T(4,128)(2,1)} fusion(bf16[16,1024]{1,0:T(8,128)(2,1)} %get-tuple-element.5), kind=kLoop, calls=%fused_computation | loop fusion | bytes 16384 | tf_op jit(solution)/shard_map/broadcast_in_dim | solution.py:649
  69.4 2.3 %copy.17 = bf16[512,1024]{1,0:T(8,128)(2,1)} copy(bf16[512,1024]{1,0:T(8,128)(2,1)} %get-tuple-element.8) | data formatting | bytes 2097152

commit v5 on v4

--- a/solution.py
+++ b/solution.py
@@ -540,7 +540,7 @@
 
     def step_unit(j):
         def first():
-            return scores(pair_keys(j), qd[...])
+            return scores(kbuf[4 * j:4 * j + 4].reshape(2 * PAIR, HD), qd[...])
 
         def second(s):
             before = topd[:1, :]
@@ -550,11 +550,12 @@
 
         def third(weights):
             w, factor = weights
-            accd[...] = accd[...] * factor + jnp.dot(pair_values(j), w, preferred_element_type=jnp.float32)
+            values = with_ones(jnp.concatenate([vbuf[4 * j + n] for n in range(4)], axis=1))
+            accd[...] = accd[...] * factor + jnp.dot(values, w, preferred_element_type=jnp.float32)
 
         return first, second, third
 
-    pipeline([step_unit(j) for j in range(8)])
+    pipeline([step_unit(j) for j in range(4)])
     mix = accd[...]
     steps = (mix[:HD] * (1.0 / mix[HD:HD + 1])).T.astype(jnp.bfloat16)
     for h in range(HEADS):

time: 71.8 us -> 71.8 us (level)
  no operation moved by 1% of the time
where the time goes in v5:
time: 71.8 us; the launch traced here: 71.6 us
  Pallas kernels  67.4 us (94%)
  local copies, waits for them, and re-layouts  3.58 us (5%)
    pallas_call x1, Pallas kernels, body(): pl.pallas_call(kernel, out_shape=(jax.ShapeDtypeStruct((ROWS, HEADS * HD)...  67.4 us
    unnamed x1, local copies, waits for them, and re-layouts  2.26 us

profile of v5, /device:TPU:18, one launch (start us, length us, event | category | flops | bytes accessed | tf_op | source)
XLA Modules:
  0.0 71.6 jit_solution(11248334890344253375)
XLA Ops:
  0.6 67.4 %shard_map.149 = (bf16[512,1024]{1,0:T(8,128)(2,1)}, bf16[16,1024]{1,0:T(8,128)(2,1)}) custom-call(bf16[512,5120]{1,0:T(8,128)(2,1)} %prompt.1, f32[1,5120]{1,0:T(1,128)} %bitcast.6, bf16[5120,1024]{1,0:T(8,128)(2,1)} %w_query.1, bf16[5120,128]{1,0:T(8,128)(2,1)} %w_key.1, bf16[5120,128]{1,0:T(8,128)(2,1)} %w_value.1, f32[1,128]{1,0:T(1,128)} %bitcast.8, ...), custom_call_target="tpu_custom_call" | custom-call | tf_op jit(solution)/shard_map/pallas_call | solution.py:608
  68.0 1.3 %slice_bitcast_fusion = bf16[1,4,1024]{2,1,0:T(4,128)(2,1)} fusion(bf16[16,1024]{1,0:T(8,128)(2,1)} %get-tuple-element.5), kind=kLoop, calls=%fused_computation | loop fusion | bytes 16384 | tf_op jit(solution)/shard_map/broadcast_in_dim | solution.py:650
  69.4 2.3 %copy.17 = bf16[512,1024]{1,0:T(8,128)(2,1)} copy(bf16[512,1024]{1,0:T(8,128)(2,1)} %get-tuple-element.8) | data formatting | bytes 2097152
